TPU v7x, 32 devices: a whole 2x2x4 slice. The times are simulated.
32 devices in a mesh: seq: 8 (over z, core), dp: 4 (over y, x).
Axes of the slice: x: 2, y: 2, z: 4, core: 2. Of those that a mesh axis runs over, the one named last changes fastest.
Arguments:
- query: bfloat16 [4096, 8192], P(('dp', 'seq')), parts along dimension 0, may hold values from -5 to 5
- keys: bfloat16 [4096, 1024], P(('dp', 'seq')), parts along dimension 0, may hold values from -7 to 7
- values: bfloat16 [4096, 1024], P(('dp', 'seq')), parts along dimension 0, may hold values from -5 to 5
- out_grad: bfloat16 [4096, 8192], P(('dp', 'seq')), parts along dimension 0, may hold values from -5 to 5
Outputs:
- attended: bfloat16 [4096, 8192], P(('dp', 'seq')), parts along dimension 0
- query_grad: bfloat16 [4096, 8192], P(('dp', 'seq')), parts along dimension 0
- key_grad: bfloat16 [4096, 1024], P(('dp', 'seq')), parts along dimension 0
- value_grad: bfloat16 [4096, 1024], P(('dp', 'seq')), parts along dimension 0
There are 4 independent parts, one for each index of `dp`. A program takes and returns all parts, laid end to end along the dimension named above; each array names one. Nothing has to cross between parts.
All inputs are finite; a program needn't handle non-finite values.
Results may differ from a plain program's by a relative error of at most 0.025.
Values may be sent and summed in bfloat16 or wider, within the bound.
No kernel may reach another device: no remote copies, remote signals or barrier semaphores. Data moves between devices by JAX's collectives and lax.ppermute only.
A program may use at most 192 MiB of HBM per device.

v0:
```python
import functools

import jax
import jax.numpy as jnp
from jax import lax
from jax.experimental import pallas as pl
from jax.experimental.pallas import tpu as pltpu
from jax.sharding import PartitionSpec as P

KVH = 8
HD = 128
CORES = 2
TOGETHER = 2
LOG2E = 1.4426950408889634
SENT = (2, 2)
CALLS = (2, 2)
BACK = (2, 2)


def dot(a, b, dims=(((1,), (0,)), ((), ()))):
    return lax.dot_general(a, b, dims, preferred_element_type=jnp.float32)


NT = (((1,), (1,)), ((), ()))


def attention_kernel(chips, heads, n_alias, place, *refs):
    q_own, q_sib, g_own, g_sib = refs[:4]
    kv = refs[4 : 4 + chips]
    outs = refs[4 + chips + n_alias :]
    att_own, dq_own, att_sib, dq_sib = outs[:4]
    dkv = outs[4 : 4 + chips]
    q_all, g_all, weights_t, grads_t, inverses = outs[4 + chips :]
    rows = q_own.shape[0]
    span = 2 * rows
    scale = HD**-0.5
    chip, core = place[0], place[1]
    wide = TOGETHER * span

    def body(blocks):
        k_t = [kv[b][0, :, :HD].T for b in range(blocks)]
        v_t = [kv[b][0, :, HD:].T for b in range(blocks)]
        key_at = lax.broadcasted_iota(jnp.int32, (span, wide), 0)
        query_at = lax.broadcasted_iota(jnp.int32, (span, wide), 1) & (span - 1)
        swap = rows * core

        def position(at):
            return jnp.where(at < rows, at + swap, at - swap)

        visible = position(query_at) >= position(key_at)
        for j in range(heads):
            lanes = slice(j * HD, (j + 1) * HD)
            q_all[j * span : j * span + rows, :] = q_own[:, lanes]
            q_all[j * span + rows : (j + 1) * span, :] = q_sib[:, lanes]
            g_all[j * span : j * span + rows, :] = g_own[:, lanes]
            g_all[j * span + rows : (j + 1) * span, :] = g_sib[:, lanes]

        def forward(i):
            columns = pl.ds(pl.multiple_of(i * wide, wide), wide)
            query = q_all[columns, :]
            scores = [dot(kv[b][0, :, :HD], query, NT) for b in range(blocks)]
            yield
            scores[0] = jnp.where(visible, scores[0], -jnp.inf)
            peak = functools.reduce(
                jnp.maximum, [jnp.max(s, axis=0, keepdims=True) for s in scores]
            )
            total = jnp.zeros((1, wide), jnp.float32)
            for b in range(blocks):
                expo = jnp.exp2((scores[b] - peak) * (scale * LOG2E))
                total += jnp.sum(expo, axis=0, keepdims=True)
                weights_t[b * span : (b + 1) * span, columns] = expo.astype(jnp.bfloat16)
            inverses[:, columns] = 1.0 / total
            yield

        def backward(i):
            columns = pl.ds(pl.multiple_of(i * wide, wide), wide)
            inverse = inverses[:, columns]
            grad_t = g_all[columns, :].T
            grad_t = (grad_t.astype(jnp.float32) * inverse).astype(jnp.bfloat16)
            g_all[columns, :] = grad_t.T
            attended_t = jnp.zeros((HD, wide), jnp.float32)
            for b in range(blocks):
                attended_t += dot(v_t[b], weights_t[b * span : (b + 1) * span, columns])
            weight_grads = [dot(kv[b][0, :, HD:], grad_t) for b in range(blocks)]
            yield
            attended_t = (attended_t * inverse).astype(jnp.bfloat16)
            row_dots = jnp.sum(
                grad_t.astype(jnp.float32) * attended_t.astype(jnp.float32),
                axis=0,
                keepdims=True,
            )
            for b in range(blocks):
                block = slice(b * span, (b + 1) * span)
                score_grads = weights_t[block, columns].astype(jnp.float32) * (
                    weight_grads[b] - row_dots
                )
                grads_t[block, columns] = score_grads.astype(jnp.bfloat16)
            yield
            query_grad_t = jnp.zeros((HD, wide), jnp.float32)
            for b in range(blocks):
                block = slice(b * span, (b + 1) * span)
                query_grad_t += dot(k_t[b], grads_t[block, columns])
            attended = attended_t.T
            query_grad = (query_grad_t * scale).astype(jnp.bfloat16).T
            for t in range(TOGETHER):
                lanes = pl.ds(pl.multiple_of((i * TOGETHER + t) * HD, HD), HD)
                own = slice(t * span, t * span + rows)
                sib = slice(t * span + rows, (t + 1) * span)
                att_own[:, lanes] = attended[own]
                att_sib[:, lanes] = attended[sib]
                dq_own[:, lanes] = query_grad[own]
                dq_sib[:, lanes] = query_grad[sib]
            yield

        def run(running, stages):
            for _ in range(stages):
                next(running)

        def paired(i, _):
            f0, f1, b0, b1 = forward(2 * i), forward(2 * i + 1), backward(2 * i), backward(2 * i + 1)
            run(f0, 1)
            run(f1, 1)
            run(f0, 1)
            run(b0, 1)
            run(f1, 1)
            run(b1, 1)
            run(b0, 1)
            run(b0, 1)
            run(b1, 2)
            return _

        lax.fori_loop(0, heads // TOGETHER // 2, paired, 0)

        for b in range(blocks):
            block = slice(b * span, (b + 1) * span)
            key_grad = dot(grads_t[block, :], q_all[...]) * scale
            value_grad = dot(weights_t[block, :], g_all[...])
            dkv[b][0, :, :HD] = key_grad.astype(dkv[b].dtype)
            dkv[b][0, :, HD:] = value_grad.astype(dkv[b].dtype)

    for c in range(chips):
        pl.when(chip == c)(functools.partial(body, c + 1))


def attention(place, first, inside, count, queries, grads, kv, carried):
    query, query_sib = queries
    grad, grad_sib = grads
    rows, width = query.shape
    group = width // KVH
    heads = group // HD
    per_core = KVH // CORES
    chips = len(kv)
    span = 2 * rows

    def full(h, s):
        return (0, s[1] * per_core + first + h)

    def half(h, s):
        return (0, first + h)

    def whole(h, s):
        return (h, 0, 0)

    def arrived(h, s):
        return (inside + h, 0, 0)

    wide = pl.BlockSpec((rows, group), full)
    narrow = pl.BlockSpec((rows, group), half)
    kv_spec = pl.BlockSpec((1, span, 2 * HD), whole)
    in_specs = [wide, narrow, wide, narrow] + [pl.BlockSpec((1, span, 2 * HD), arrived)] * chips
    in_specs += [pl.BlockSpec(memory_space=pl.ANY)] * len(carried)
    half_width = width // CORES
    bf = jnp.bfloat16
    out_shape = [
        jax.ShapeDtypeStruct((rows, width), bf),
        jax.ShapeDtypeStruct((rows, width), bf),
        jax.ShapeDtypeStruct((rows, half_width), bf),
        jax.ShapeDtypeStruct((rows, half_width), bf),
    ] + [
        jax.ShapeDtypeStruct((count, span, 2 * HD), jnp.float32 if b == 0 else bf)
        for b in range(chips)
    ]
    out_specs = [wide, wide, narrow, narrow] + [kv_spec] * chips
    first_carried = 1 + 4 + chips
    results = pl.pallas_call(
        functools.partial(attention_kernel, chips, heads, len(carried)),
        grid_spec=pltpu.PrefetchScalarGridSpec(
            num_scalar_prefetch=1,
            grid=(count,),
            in_specs=in_specs,
            out_specs=out_specs,
            scratch_shapes=[
                pltpu.VMEM((heads * span, HD), bf),
                pltpu.VMEM((heads * span, HD), bf),
                pltpu.VMEM((chips * span, heads * span), bf),
                pltpu.VMEM((chips * span, heads * span), bf),
                pltpu.VMEM((1, heads * span), jnp.float32),
            ],
        ),
        out_shape=out_shape,
        input_output_aliases={first_carried + i: i for i in range(len(carried))},
        compiler_params=pltpu.CompilerParams(vmem_limit_bytes=52 * 2**20),
        cost_estimate=pl.CostEstimate(
            flops=count * 12 * heads * span * span * chips * HD,
            bytes_accessed=count * (8 * rows * group * 2 + 2 * chips * span * 2 * HD * 2),
            transcendentals=count * heads * span * span * chips,
        ),
        name=f"attention_{first}",
    )(place, query, query_sib, grad, grad_sib, *kv, *carried)
    return results[:4], results[4:]


def shards(query, keys, values, out_grad):
    devices = lax.axis_size("seq")
    chips = devices // CORES
    rows = query.shape[0]
    me = lax.axis_index("seq")
    chip, core = me // CORES, me % CORES
    place = jnp.stack([chip, core]).astype(jnp.int32)
    per_core = KVH // CORES
    sibling = [(i, i ^ 1) for i in range(devices)]

    def onward(d):
        return [(i, i + CORES * d) for i in range(devices - CORES * d)]

    def back(d):
        return [(i + CORES * d, i) for i in range(devices - CORES * d)]

    packed = jnp.stack(
        [
            jnp.concatenate(
                [keys[:, h * HD : (h + 1) * HD], values[:, h * HD : (h + 1) * HD]], 1
            )
            for h in range(KVH)
        ]
    )
    mine = lax.dynamic_slice_in_dim(packed, core * per_core, per_core, 0)
    theirs = lax.dynamic_slice_in_dim(packed, (1 - core) * per_core, per_core, 0)
    kv_own = jnp.concatenate([mine, lax.ppermute(theirs, "seq", sibling)], 1)

    kv = {}
    first = 0
    for count in SENT:
        part = kv_own[first : first + count]
        blocks = [part] + [lax.ppermute(part, "seq", onward(d)) for d in range(chips - 1, 0, -1)][::-1]
        for h in range(count):
            kv[first + h] = (h, blocks)
        first += count

    half = query.shape[1] // CORES
    kv_own, late_query, late_grad = lax.optimization_barrier((kv_own, query, out_grad))

    def other(tensor):
        piece = lax.dynamic_slice_in_dim(tensor, (1 - core) * half, half, 1)
        return lax.ppermute(piece, "seq", sibling)

    query_sib, grad_sib = other(late_query), other(late_grad)

    carried = ()
    parts = []
    first = 0
    for count in CALLS:
        inside, blocks = kv[first]
        carried, dkv = attention(
            place, first, inside, count, (query, query_sib), (out_grad, grad_sib), blocks, carried
        )
        parts += [[d[h : h + 1] for d in dkv] for h in range(count)]
        first += count

    attended, query_grad, att_sib, dq_sib = carried

    totals = []
    first = 0
    for count in BACK:
        group = [
            jnp.concatenate([parts[h][d] for h in range(first, first + count)], 0)
            for d in range(chips)
        ]
        total = group[0]
        for d in range(chips - 1, 0, -1):
            total = total + lax.ppermute(group[d], "seq", back(d)).astype(jnp.float32)
        total = total.astype(jnp.bfloat16)
        arrived = lax.ppermute(total[:, rows:], "seq", sibling)
        totals.append((total[:, :rows], arrived))
        first += count

    def placed_back(tensor, piece):
        arrived = lax.ppermute(piece, "seq", sibling)
        return lax.dynamic_update_slice_in_dim(tensor, arrived, (1 - core) * half, 1)

    attended = placed_back(attended, att_sib)
    query_grad = placed_back(query_grad, dq_sib)

    ours = [o[h] for o, _ in totals for h in range(o.shape[0])]
    arrived = [a[h] for _, a in totals for h in range(a.shape[0])]
    low = [jnp.where(core == 0, o, a) for o, a in zip(ours, arrived)]
    high = [jnp.where(core == 0, a, o) for o, a in zip(ours, arrived)]
    both = low + high
    key_grad = jnp.concatenate([b[:, :HD] for b in both], 1)
    value_grad = jnp.concatenate([b[:, HD:] for b in both], 1)
    return attended, query_grad, key_grad, value_grad


def solution(mesh):
    spec = P(("dp", "seq"), None)
    return jax.shard_map(
        shards, mesh=mesh, in_specs=(spec,) * 4, out_specs=(spec,) * 4, check_vma=False
    )
```

profile of v0, /device:TPU:9, one launch (start us, length us, event | category | flops | bytes accessed | tf_op | source)
XLA Modules:
  0.0 117.5 jit_solution(12991565960960968992)
XLA Ops:
  0.7 0.0 copy-start.2
  0.7 0.0 copy-start.3
  0.7 0.0 copy-start.4
  0.7 1.4 %constant_dynamic-slice_fusion = bf16[128,4096]{1,0:T(8,128)(2,1)S(1)} fusion(bf16[128,8192]{1,0:T(8,128)(2,1)} %refs_2_.3, s32[]{:T(128)S(6)} %select_n.87), kind=kLoop, calls=%fused_computation.51 | loop fusion | bytes 2097156 | tf_op jit(solution)/shard_map/dynamic_slice | solution.py:254
  2.1 0.7 collective-permute-start.2
  2.9 0.0 copy-done.2
  2.9 0.1 constant_dynamic-slice_fusion.1
  3.0 0.4 collective-permute-start.1
  3.4 0.0 copy-done.3
  3.4 0.0 copy-done.4
  3.4 0.1 fusion.10
  3.7 0.2 collective-permute-start
  3.9 2.0 %collective-permute-done = bf16[4,128,256]{2,1,0:T(8,128)(2,1)S(1)} collective-permute-done((bf16[4,128,256]{2,1,0:T(8,128)(2,1)S(1)}, bf16[4,128,256]{2,1,0:T(8,128)(2,1)S(1)}, u32[]{:S(2)}, u32[]{:S(2)}) %collective-permute-start) | collective-permute-done | bytes 262176 | tf_op jit(solution)/shard_map/ppermute | solution.py:239
  5.9 0.7 collective-permute-start.8
  6.6 4.8 %collective-permute-start.7 = (bf16[2,256,256]{2,1,0:T(8,128)(2,1)S(1)}, bf16[2,256,256]{2,1,0:T(8,128)(2,1)S(1)}, u32[]{:S(2)}, u32[]{:S(2)}) collective-permute-start(bf16[2,256,256]{2,1,0:T(8,128)(2,1)S(1)} %get-tuple-element.40.refs_4_), channel_id=1, source_target_pairs={{0,16},{4,20},{8,24},{12,28},{1,17},{5,21},{9,25},{13,29},{2,18},{... | collective-permute-start | bytes 786440 | tf_op jit(solution)/shard_map/ppermute | solution.py:245
  11.5 1.9 %collective-permute-start.6 = (bf16[2,256,256]{2,1,0:T(8,128)(2,1)S(1)}, bf16[2,256,256]{2,1,0:T(8,128)(2,1)S(1)}, u32[]{:S(2)}, u32[]{:S(2)}) collective-permute-start(bf16[2,256,256]{2,1,0:T(8,128)(2,1)S(1)} %get-tuple-element.40.refs_4_), channel_id=1, source_target_pairs={{0,8},{4,12},{8,16},{12,20},{16,24},{20,28},{1,9},{5,13},{9,17},{1... | collective-permute-start | bytes 786440 | tf_op jit(solution)/shard_map/ppermute | solution.py:245
  13.4 0.1 pad_add_fusion.place
  13.5 0.0 collective-permute-done.8.refs_7_
  13.5 0.7 collective-permute-start.5
  14.2 14.4 %collective-permute-done.7.refs_6_ = bf16[2,256,256]{2,1,0:T(8,128)(2,1)S(1)} collective-permute-done((bf16[2,256,256]{2,1,0:T(8,128)(2,1)S(1)}, bf16[2,256,256]{2,1,0:T(8,128)(2,1)S(1)}, u32[]{:S(2)}, u32[]{:S(2)}) %collective-permute-start.7) | collective-permute-done | bytes 262176 | tf_op jit(solution)/shard_map/ppermute | solution.py:245
  28.6 5.5 %collective-permute-start.4 = (bf16[2,256,256]{2,1,0:T(8,128)(2,1)S(1)}, bf16[2,256,256]{2,1,0:T(8,128)(2,1)S(1)}, u32[]{:S(2)}, u32[]{:S(2)}) collective-permute-start(bf16[2,256,256]{2,1,0:T(8,128)(2,1)S(1)} %get-tuple-element.41.refs_4_), channel_id=1, source_target_pairs={{0,16},{4,20},{8,24},{12,28},{1,17},{5,21},{9,25},{13,29},{2,18},{... | collective-permute-start | bytes 786440 | tf_op jit(solution)/shard_map/ppermute | solution.py:245
  34.1 11.2 %collective-permute-done.6.refs_5_ = bf16[2,256,256]{2,1,0:T(8,128)(2,1)S(1)} collective-permute-done((bf16[2,256,256]{2,1,0:T(8,128)(2,1)S(1)}, bf16[2,256,256]{2,1,0:T(8,128)(2,1)S(1)}, u32[]{:S(2)}, u32[]{:S(2)}) %collective-permute-start.6) | collective-permute-done | bytes 262176 | tf_op jit(solution)/shard_map/ppermute | solution.py:245
  45.2 4.1 %collective-permute-start.3 = (bf16[2,256,256]{2,1,0:T(8,128)(2,1)S(1)}, bf16[2,256,256]{2,1,0:T(8,128)(2,1)S(1)}, u32[]{:S(2)}, u32[]{:S(2)}) collective-permute-start(bf16[2,256,256]{2,1,0:T(8,128)(2,1)S(1)} %get-tuple-element.41.refs_4_), channel_id=1, source_target_pairs={{0,8},{4,12},{8,16},{12,20},{16,24},{20,28},{1,9},{5,13},{9,17},{1... | collective-permute-start | bytes 786440 | tf_op jit(solution)/shard_map/ppermute | solution.py:245
  49.3 0.0 collective-permute-done.2.refs_3_
  49.3 0.0 collective-permute-done.1.refs_1_
  49.4 13.0 %attention_0.1 = (bf16[128,8192]{1,0:T(8,128)(2,1)}, bf16[128,8192]{1,0:T(8,128)(2,1)}, bf16[128,4096]{1,0:T(8,128)(2,1)}, bf16[128,4096]{1,0:T(8,128)(2,1)}, f3...) custom-call(s32[2]{0:T(128)S(1)} %pad_add_fusion.place, ...), custom_call_target="tpu_custom_call" | custom-call | flops 6442450944 | bytes 6291456 | tf_op jit(solution)/shard_map/attention_0/pallas_call | solution.py:185
  62.4 0.7 collective-permute-start.11
  63.1 1.3 %collective-permute-start.12 = (bf16[2,256,256]{2,1,0:T(8,128)(2,1)S(1)}, bf16[2,256,256]{2,1,0:T(8,128)(2,1)S(1)}, u32[]{:S(2)}, u32[]{:S(2)}) collective-permute-start(bf16[2,256,256]{2,1,0:T(8,128)(2,1)S(1)} %get-tuple-element.34), channel_id=1, source_target_pairs={{16,0},{20,4},{24,8},{28,12},{17,1},{21,5},{25,9},{29,13},{18,2},{... | collective-permute-start | bytes 786440 | tf_op jit(solution)/shard_map/ppermute | solution.py:281
  64.4 0.0 collective-permute-done.5.refs_7_
  64.4 1.9 %collective-permute-start.13 = (bf16[2,256,256]{2,1,0:T(8,128)(2,1)S(1)}, bf16[2,256,256]{2,1,0:T(8,128)(2,1)S(1)}, u32[]{:S(2)}, u32[]{:S(2)}) collective-permute-start(bf16[2,256,256]{2,1,0:T(8,128)(2,1)S(1)} %get-tuple-element.35), channel_id=1, source_target_pairs={{8,0},{12,4},{16,8},{20,12},{24,16},{28,20},{9,1},{13,5},{17,9},{2... | collective-permute-start | bytes 786440 | tf_op jit(solution)/shard_map/ppermute | solution.py:281
  66.3 0.0 collective-permute-done.4.refs_6_
  66.3 0.0 collective-permute-done.3.refs_5_
  66.3 0.0 copy-start
  66.3 13.3 %attention_2.1 = (bf16[128,8192]{1,0:T(8,128)(2,1)}, bf16[128,8192]{1,0:T(8,128)(2,1)}, bf16[128,4096]{1,0:T(8,128)(2,1)}, bf16[128,4096]{1,0:T(8,128)(2,1)}, f3...) custom-call(s32[2]{0:T(128)S(1)} %pad_add_fusion.place, ...), custom_call_target="tpu_custom_call", output_to_operand_aliasing={{0}: (9, {}), {1}: (10, {}), {2}: (11, {}), {3}: (12, {})} | custom-call | flops 6442450944 | bytes 6291456 | tf_op jit(solution)/shard_map/attention_2/pallas_call | solution.py:185
  79.6 0.8 collective-permute-start.15
  80.4 1.3 %collective-permute-start.16 = (bf16[2,256,256]{2,1,0:T(8,128)(2,1)S(1)}, bf16[2,256,256]{2,1,0:T(8,128)(2,1)S(1)}, u32[]{:S(2)}, u32[]{:S(2)}) collective-permute-start(bf16[2,256,256]{2,1,0:T(8,128)(2,1)S(1)} %get-tuple-element.38), channel_id=1, source_target_pairs={{16,0},{20,4},{24,8},{28,12},{17,1},{21,5},{25,9},{29,13},{18,2},{... | collective-permute-start | bytes 786440 | tf_op jit(solution)/shard_map/ppermute | solution.py:281
  81.7 0.0 collective-permute-done.11
  81.7 1.9 %collective-permute-start.17 = (bf16[2,256,256]{2,1,0:T(8,128)(2,1)S(1)}, bf16[2,256,256]{2,1,0:T(8,128)(2,1)S(1)}, u32[]{:S(2)}, u32[]{:S(2)}) collective-permute-start(bf16[2,256,256]{2,1,0:T(8,128)(2,1)S(1)} %get-tuple-element.39), channel_id=1, source_target_pairs={{8,0},{12,4},{16,8},{20,12},{24,16},{28,20},{9,1},{13,5},{17,9},{2... | collective-permute-start | bytes 786440 | tf_op jit(solution)/shard_map/ppermute | solution.py:281
  83.7 0.0 collective-permute-done.12
  83.7 0.9 collective-permute-start.9
  84.6 1.1 collective-permute-done.13
  85.7 0.5 collective-permute-start.10
  86.2 0.1 add_convert_fusion.1
  86.3 0.0 copy-start.7
  86.3 0.0 collective-permute-done.15
  86.3 0.1 collective-permute-start.14
  86.4 19.1 %collective-permute-done.16 = bf16[2,256,256]{2,1,0:T(8,128)(2,1)S(1)} collective-permute-done((bf16[2,256,256]{2,1,0:T(8,128)(2,1)S(1)}, bf16[2,256,256]{2,1,0:T(8,128)(2,1)S(1)}, u32[]{:S(2)}, u32[]{:S(2)}) %collective-permute-start.16) | collective-permute-done | bytes 262176 | tf_op jit(solution)/shard_map/ppermute | solution.py:281
  105.6 7.3 %collective-permute-done.17 = bf16[2,256,256]{2,1,0:T(8,128)(2,1)S(1)} collective-permute-done((bf16[2,256,256]{2,1,0:T(8,128)(2,1)S(1)}, bf16[2,256,256]{2,1,0:T(8,128)(2,1)S(1)}, u32[]{:S(2)}, u32[]{:S(2)}) %collective-permute-start.17) | collective-permute-done | bytes 262176 | tf_op jit(solution)/shard_map/ppermute | solution.py:281
  112.8 0.1 add_convert_fusion
  113.0 1.2 collective-permute-start.18
  114.2 0.0 collective-permute-done.14
  114.3 0.9 collective-permute-done.18
  115.4 0.0 copy-start.5
  115.4 0.0 copy-start.6
  115.4 0.0 collective-permute-done.9
  115.4 0.0 copy-done.7
  115.4 0.1 constant_dynamic-update-slice_fusion.17
  115.5 0.0 copy-start.8
  115.5 0.0 collective-permute-done.10
  115.6 0.1 constant_dynamic-update-slice_fusion.16
  115.7 0.4 copy-done.5
  116.1 0.1 copy-done.6
  116.2 0.7 copy-done.8
  116.9 0.7 copy-done.10
  (28 shorter events, 0.4 us)
Async XLA Ops:
  0.7 2.2 %copy-start.2 = (bf16[128,8192]{1,0:T(8,128)(2,1)S(1)}, bf16[128,8192]{1,0:T(8,128)(2,1)}, u32[]{:S(2)}) copy-start(bf16[128,8192]{1,0:T(8,128)(2,1)} %refs_0_.3) | copy-start | bytes 6291460
  0.7 2.7 %copy-start.3 = (bf16[128,1024]{1,0:T(8,128)(2,1)S(1)}, bf16[128,1024]{1,0:T(8,128)(2,1)}, u32[]{:S(2)}) copy-start(bf16[128,1024]{1,0:T(8,128)(2,1)} %param.5) | copy-start | bytes 786436
  0.7 2.7 %copy-start.4 = (bf16[128,1024]{1,0:T(8,128)(2,1)S(1)}, bf16[128,1024]{1,0:T(8,128)(2,1)}, u32[]{:S(2)}) copy-start(bf16[128,1024]{1,0:T(8,128)(2,1)} %param.6) | copy-start | bytes 786436
  2.1 47.2 %collective-permute-start.2 = (bf16[128,4096]{1,0:T(8,128)(2,1)S(1)}, bf16[128,4096]{1,0:T(8,128)(2,1)}, u32[]{:S(2)}, u32[]{:S(2)}) collective-permute-start(bf16[128,4096]{1,0:T(8,128)(2,1)S(1)} %constant_dynamic-slice_fusion), channel_id=1, source_target_pairs={{0,4},{4,0},{8,12},{12,8},{16,20},{20,16},{24,28},{28,24},{1,5},{5... | collective-permute-start | bytes 3145736 | tf_op jit(solution)/shard_map/ppermute | solution.py:255
  3.0 46.4 %collective-permute-start.1 = (bf16[128,4096]{1,0:T(8,128)(2,1)S(1)}, bf16[128,4096]{1,0:T(8,128)(2,1)}, u32[]{:S(2)}, u32[]{:S(2)}) collective-permute-start(bf16[128,4096]{1,0:T(8,128)(2,1)S(1)} %constant_dynamic-slice_fusion.1), channel_id=1, source_target_pairs={{0,4},{4,0},{8,12},{12,8},{16,20},{20,16},{24,28},{28,24},{1,5},{5... | collective-permute-start | bytes 3145736 | tf_op jit(solution)/shard_map/ppermute | solution.py:255
  3.7 2.2 %collective-permute-start = (bf16[4,128,256]{2,1,0:T(8,128)(2,1)S(1)}, bf16[4,128,256]{2,1,0:T(8,128)(2,1)S(1)}, u32[]{:S(2)}, u32[]{:S(2)}) collective-permute-start(bf16[4,128,256]{2,1,0:T(8,128)(2,1)S(1)} %get-tuple-element.42), channel_id=1, source_target_pairs={{0,4},{4,0},{8,12},{12,8},{16,20},{20,16},{24,28},{28,24},{1,5},{5... | collective-permute-start | bytes 786440 | tf_op jit(solution)/shard_map/ppermute | solution.py:239
  5.9 7.6 %collective-permute-start.8 = (bf16[2,256,256]{2,1,0:T(8,128)(2,1)S(1)}, bf16[2,256,256]{2,1,0:T(8,128)(2,1)S(1)}, u32[]{:S(2)}, u32[]{:S(2)}) collective-permute-start(bf16[2,256,256]{2,1,0:T(8,128)(2,1)S(1)} %get-tuple-element.40.refs_4_), channel_id=1, source_target_pairs={{0,24},{4,28},{1,25},{5,29},{2,26},{6,30},{3,27},{7,31}} | collective-permute-start | bytes 786440 | tf_op jit(solution)/shard_map/ppermute | solution.py:245
  6.6 21.9 %collective-permute-start.7 = (bf16[2,256,256]{2,1,0:T(8,128)(2,1)S(1)}, bf16[2,256,256]{2,1,0:T(8,128)(2,1)S(1)}, u32[]{:S(2)}, u32[]{:S(2)}) collective-permute-start(bf16[2,256,256]{2,1,0:T(8,128)(2,1)S(1)} %get-tuple-element.40.refs_4_), channel_id=1, source_target_pairs={{0,16},{4,20},{8,24},{12,28},{1,17},{5,21},{9,25},{13,29},{2,18},{... | collective-permute-start | bytes 786440 | tf_op jit(solution)/shard_map/ppermute | solution.py:245
  11.5 33.7 %collective-permute-start.6 = (bf16[2,256,256]{2,1,0:T(8,128)(2,1)S(1)}, bf16[2,256,256]{2,1,0:T(8,128)(2,1)S(1)}, u32[]{:S(2)}, u32[]{:S(2)}) collective-permute-start(bf16[2,256,256]{2,1,0:T(8,128)(2,1)S(1)} %get-tuple-element.40.refs_4_), channel_id=1, source_target_pairs={{0,8},{4,12},{8,16},{12,20},{16,24},{20,28},{1,9},{5,13},{9,17},{1... | collective-permute-start | bytes 786440 | tf_op jit(solution)/shard_map/ppermute | solution.py:245
  13.5 50.9 %collective-permute-start.5 = (bf16[2,256,256]{2,1,0:T(8,128)(2,1)S(1)}, bf16[2,256,256]{2,1,0:T(8,128)(2,1)S(1)}, u32[]{:S(2)}, u32[]{:S(2)}) collective-permute-start(bf16[2,256,256]{2,1,0:T(8,128)(2,1)S(1)} %get-tuple-element.41.refs_4_), channel_id=1, source_target_pairs={{0,24},{4,28},{1,25},{5,29},{2,26},{6,30},{3,27},{7,31}} | collective-permute-start | bytes 786440 | tf_op jit(solution)/shard_map/ppermute | solution.py:245
  28.6 37.8 %collective-permute-start.4 = (bf16[2,256,256]{2,1,0:T(8,128)(2,1)S(1)}, bf16[2,256,256]{2,1,0:T(8,128)(2,1)S(1)}, u32[]{:S(2)}, u32[]{:S(2)}) collective-permute-start(bf16[2,256,256]{2,1,0:T(8,128)(2,1)S(1)} %get-tuple-element.41.refs_4_), channel_id=1, source_target_pairs={{0,16},{4,20},{8,24},{12,28},{1,17},{5,21},{9,25},{13,29},{2,18},{... | collective-permute-start | bytes 786440 | tf_op jit(solution)/shard_map/ppermute | solution.py:245
  45.2 21.1 %collective-permute-start.3 = (bf16[2,256,256]{2,1,0:T(8,128)(2,1)S(1)}, bf16[2,256,256]{2,1,0:T(8,128)(2,1)S(1)}, u32[]{:S(2)}, u32[]{:S(2)}) collective-permute-start(bf16[2,256,256]{2,1,0:T(8,128)(2,1)S(1)} %get-tuple-element.41.refs_4_), channel_id=1, source_target_pairs={{0,8},{4,12},{8,16},{12,20},{16,24},{20,28},{1,9},{5,13},{9,17},{1... | collective-permute-start | bytes 786440 | tf_op jit(solution)/shard_map/ppermute | solution.py:245
  62.4 19.3 %collective-permute-start.11 = (bf16[2,256,256]{2,1,0:T(8,128)(2,1)S(1)}, bf16[2,256,256]{2,1,0:T(8,128)(2,1)S(1)}, u32[]{:S(2)}, u32[]{:S(2)}) collective-permute-start(bf16[2,256,256]{2,1,0:T(8,128)(2,1)S(1)} %get-tuple-element.33), channel_id=1, source_target_pairs={{24,0},{28,4},{25,1},{29,5},{26,2},{30,6},{27,3},{31,7}} | collective-permute-start | bytes 786440 | tf_op jit(solution)/shard_map/ppermute | solution.py:281
  63.1 20.6 %collective-permute-start.12 = (bf16[2,256,256]{2,1,0:T(8,128)(2,1)S(1)}, bf16[2,256,256]{2,1,0:T(8,128)(2,1)S(1)}, u32[]{:S(2)}, u32[]{:S(2)}) collective-permute-start(bf16[2,256,256]{2,1,0:T(8,128)(2,1)S(1)} %get-tuple-element.34), channel_id=1, source_target_pairs={{16,0},{20,4},{24,8},{28,12},{17,1},{21,5},{25,9},{29,13},{18,2},{... | collective-permute-start | bytes 786440 | tf_op jit(solution)/shard_map/ppermute | solution.py:281
  64.4 21.3 %collective-permute-start.13 = (bf16[2,256,256]{2,1,0:T(8,128)(2,1)S(1)}, bf16[2,256,256]{2,1,0:T(8,128)(2,1)S(1)}, u32[]{:S(2)}, u32[]{:S(2)}) collective-permute-start(bf16[2,256,256]{2,1,0:T(8,128)(2,1)S(1)} %get-tuple-element.35), channel_id=1, source_target_pairs={{8,0},{12,4},{16,8},{20,12},{24,16},{28,20},{9,1},{13,5},{17,9},{2... | collective-permute-start | bytes 786440 | tf_op jit(solution)/shard_map/ppermute | solution.py:281
  66.3 19.8 %copy-start = (f32[2,256,256]{2,1,0:T(8,128)S(1)}, f32[2,256,256]{2,1,0:T(8,128)}, u32[]{:S(2)}) copy-start(f32[2,256,256]{2,1,0:T(8,128)} %get-tuple-element.32) | copy-start | bytes 1572868
  79.6 33.2 %copy-start.1 = (f32[2,256,256]{2,1,0:T(8,128)S(1)}, f32[2,256,256]{2,1,0:T(8,128)}, u32[]{:S(2)}) copy-start(f32[2,256,256]{2,1,0:T(8,128)} %get-tuple-element.36) | copy-start | bytes 1572868
  79.6 6.7 %collective-permute-start.15 = (bf16[2,256,256]{2,1,0:T(8,128)(2,1)S(1)}, bf16[2,256,256]{2,1,0:T(8,128)(2,1)S(1)}, u32[]{:S(2)}, u32[]{:S(2)}) collective-permute-start(bf16[2,256,256]{2,1,0:T(8,128)(2,1)S(1)} %get-tuple-element.37), channel_id=1, source_target_pairs={{24,0},{28,4},{25,1},{29,5},{26,2},{30,6},{27,3},{31,7}} | collective-permute-start | bytes 786440 | tf_op jit(solution)/shard_map/ppermute | solution.py:281
  80.4 25.1 %collective-permute-start.16 = (bf16[2,256,256]{2,1,0:T(8,128)(2,1)S(1)}, bf16[2,256,256]{2,1,0:T(8,128)(2,1)S(1)}, u32[]{:S(2)}, u32[]{:S(2)}) collective-permute-start(bf16[2,256,256]{2,1,0:T(8,128)(2,1)S(1)} %get-tuple-element.38), channel_id=1, source_target_pairs={{16,0},{20,4},{24,8},{28,12},{17,1},{21,5},{25,9},{29,13},{18,2},{... | collective-permute-start | bytes 786440 | tf_op jit(solution)/shard_map/ppermute | solution.py:281
  81.7 31.1 %collective-permute-start.17 = (bf16[2,256,256]{2,1,0:T(8,128)(2,1)S(1)}, bf16[2,256,256]{2,1,0:T(8,128)(2,1)S(1)}, u32[]{:S(2)}, u32[]{:S(2)}) collective-permute-start(bf16[2,256,256]{2,1,0:T(8,128)(2,1)S(1)} %get-tuple-element.39), channel_id=1, source_target_pairs={{8,0},{12,4},{16,8},{20,12},{24,16},{28,20},{9,1},{13,5},{17,9},{2... | collective-permute-start | bytes 786440 | tf_op jit(solution)/shard_map/ppermute | solution.py:281
  83.7 31.7 %collective-permute-start.9 = (bf16[128,4096]{1,0:T(8,128)(2,1)}, bf16[128,4096]{1,0:T(8,128)(2,1)S(1)}, u32[]{:S(2)}, u32[]{:S(2)}) collective-permute-start(bf16[128,4096]{1,0:T(8,128)(2,1)} %get-tuple-element.29), channel_id=1, source_target_pairs={{0,4},{4,0},{8,12},{12,8},{16,20},{20,16},{24,28},{28,24},{1,5},{5... | collective-permute-start | bytes 3145736 | tf_op jit(solution)/shard_map/ppermute | solution.py:288
  85.7 29.8 %collective-permute-start.10 = (bf16[128,4096]{1,0:T(8,128)(2,1)}, bf16[128,4096]{1,0:T(8,128)(2,1)S(1)}, u32[]{:S(2)}, u32[]{:S(2)}) collective-permute-start(bf16[128,4096]{1,0:T(8,128)(2,1)} %get-tuple-element.31), channel_id=1, source_target_pairs={{0,4},{4,0},{8,12},{12,8},{16,20},{20,16},{24,28},{28,24},{1,5},{5... | collective-permute-start | bytes 3145736 | tf_op jit(solution)/shard_map/ppermute | solution.py:288
  86.3 29.1 %copy-start.7 = (bf16[128,8192]{1,0:T(8,128)(2,1)S(1)}, bf16[128,8192]{1,0:T(8,128)(2,1)}, u32[]{:S(2)}) copy-start(bf16[128,8192]{1,0:T(8,128)(2,1)} %get-tuple-element.28) | copy-start | bytes 6291460
  86.3 27.9 %collective-permute-start.14 = (bf16[2,128,256]{2,1,0:T(8,128)(2,1)S(1)}, bf16[2,128,256]{2,1,0:T(8,128)(2,1)S(1)}, u32[]{:S(2)}, u32[]{:S(2)}) collective-permute-start(bf16[2,128,256]{2,1,0:T(8,128)(2,1)S(1)} %slice.211), channel_id=1, source_target_pairs={{0,4},{4,0},{8,12},{12,8},{16,20},{20,16},{24,28},{28,24},{1,5},{5... | collective-permute-start | bytes 393224 | tf_op jit(solution)/shard_map/ppermute | solution.py:283
  113.0 2.5 %copy-start.9 = (bf16[128,8192]{1,0:T(8,128)(2,1)S(1)}, bf16[128,8192]{1,0:T(8,128)(2,1)}, u32[]{:S(2)}) copy-start(bf16[128,8192]{1,0:T(8,128)(2,1)} %get-tuple-element.30) | copy-start | bytes 6291460
  113.0 2.2 %collective-permute-start.18 = (bf16[2,128,256]{2,1,0:T(8,128)(2,1)S(1)}, bf16[2,128,256]{2,1,0:T(8,128)(2,1)S(1)}, u32[]{:S(2)}, u32[]{:S(2)}) collective-permute-start(bf16[2,128,256]{2,1,0:T(8,128)(2,1)S(1)} %slice.218), channel_id=1, source_target_pairs={{0,4},{4,0},{8,12},{12,8},{16,20},{20,16},{24,28},{28,24},{1,5},{5... | collective-permute-start | bytes 393224 | tf_op jit(solution)/shard_map/ppermute | solution.py:283
  115.4 0.7 copy-start.5
  115.4 0.8 copy-start.6
  115.5 1.3 %copy-start.8 = (bf16[128,8192]{1,0:T(8,128)(2,1)}, bf16[128,8192]{1,0:T(8,128)(2,1)S(1)}, u32[]{:S(2)}) copy-start(bf16[128,8192]{1,0:T(8,128)(2,1)S(1)} %constant_dynamic-update-slice_fusion.17) | copy-start | bytes 6291460
  116.2 1.4 %copy-start.10 = (bf16[128,8192]{1,0:T(8,128)(2,1)}, bf16[128,8192]{1,0:T(8,128)(2,1)S(1)}, u32[]{:S(2)}) copy-start(bf16[128,8192]{1,0:T(8,128)(2,1)S(1)} %constant_dynamic-update-slice_fusion.16) | copy-start | bytes 6291460
where the time goes:
time: 118 us
  waiting for transfers between devices  55.9 us (47%)
  starting transfers between devices  29.6 us (25%)
  Pallas kernels  26.3 us (22%)
  local copies, waits for them, and re-layouts  4 us (3%)
    ppermute x6, waiting for transfers between devices, shards(): total = total + lax.ppermute(group[d], 'seq', back(d)).astype(jnp.float32)  27.5 us
    pallas_call x2, Pallas kernels, attention(): pl.pallas_call(functools.partial(attention_kernel, chips, heads, len(carr...  26.3 us
    ppermute x6, waiting for transfers between devices, shards(): lax.ppermute(part, 'seq', onward(d))  25.5 us
    ppermute x6, starting transfers between devices, shards(): lax.ppermute(part, 'seq', onward(d))  17.7 us
    ppermute x6, starting transfers between devices, shards(): total = total + lax.ppermute(group[d], 'seq', back(d)).astype(jnp.float32)  7.89 us
  transfers between devices with their start and end apart: 19, of which 7 were waited for; matrix products, arithmetic and copies ran while one was open for 1% of the time, Pallas kernels for 22%

commit v1 on v0

--- a/solution.py
+++ b/solution.py
@@ -238,23 +238,25 @@
     theirs = lax.dynamic_slice_in_dim(packed, (1 - core) * per_core, per_core, 0)
     kv_own = jnp.concatenate([mine, lax.ppermute(theirs, "seq", sibling)], 1)
 
+    half = query.shape[1] // CORES
+
+    def other(tensor):
+        piece = lax.dynamic_slice_in_dim(tensor, (1 - core) * half, half, 1)
+        return lax.ppermute(piece, "seq", sibling)
+
+    query_sib, grad_sib = other(query), other(out_grad)
+
     kv = {}
     first = 0
     for count in SENT:
         part = kv_own[first : first + count]
-        blocks = [part] + [lax.ppermute(part, "seq", onward(d)) for d in range(chips - 1, 0, -1)][::-1]
+        if first:
+            part, *arrived = lax.optimization_barrier((part, *blocks[1:]))
+            blocks[1:] = arrived
+        blocks = [part] + [lax.ppermute(part, "seq", onward(d)) for d in range(1, chips)]
         for h in range(count):
             kv[first + h] = (h, blocks)
         first += count
-
-    half = query.shape[1] // CORES
-    kv_own, late_query, late_grad = lax.optimization_barrier((kv_own, query, out_grad))
-
-    def other(tensor):
-        piece = lax.dynamic_slice_in_dim(tensor, (1 - core) * half, half, 1)
-        return lax.ppermute(piece, "seq", sibling)
-
-    query_sib, grad_sib = other(late_query), other(late_grad)
 
     carried = ()
     parts = []
@@ -269,20 +271,27 @@
 
     attended, query_grad, att_sib, dq_sib = carried
 
-    totals = []
+    returned = []
     first = 0
     for count in BACK:
         group = [
             jnp.concatenate([parts[h][d] for h in range(first, first + count)], 0)
             for d in range(chips)
         ]
+        returned.append(
+            [group[0]] + [lax.ppermute(group[d], "seq", back(d)) for d in range(1, chips)]
+        )
+        first += count
+    returned[:-1], att_sib = lax.optimization_barrier((returned[:-1], att_sib))
+
+    totals = []
+    for group in returned:
         total = group[0]
         for d in range(chips - 1, 0, -1):
-            total = total + lax.ppermute(group[d], "seq", back(d)).astype(jnp.float32)
+            total = total + group[d].astype(jnp.float32)
         total = total.astype(jnp.bfloat16)
         arrived = lax.ppermute(total[:, rows:], "seq", sibling)
         totals.append((total[:, :rows], arrived))
-        first += count
 
     def placed_back(tensor, piece):
         arrived = lax.ppermute(piece, "seq", sibling)

time: 118 us -> 111 us (0.941)
  starting transfers between devices: 29.6 us -> 24.8 us
  waiting for transfers between devices: 55.9 us -> 53.9 us
    ppermute x6, waiting for transfers between devices: 25.5 us -> 20.6 us  [shards(): lax.ppermute(part, 'seq', onward(d))]
    ppermute x6, starting transfers between devices: 17.7 us -> 13.5 us  [shards(): lax.ppermute(part, 'seq', onward(d))]
    ppermute x6, waiting for transfers between devices: 27.5 us -> 29.2 us  [shards(): lax.ppermute(group[d], 'seq', back(d))]
    ppermute x2, waiting for transfers between devices: 0.01 us -> 1.32 us  [placed_back(): arrived = lax.ppermute(piece, 'seq', sibling)]
  transfers between devices with their start and end apart: 19 -> 19, of which waited for: 7 -> 8; matrix products, arithmetic and copies ran while one was open for 1% -> 1% of each run, Pallas kernels for 22% -> 24%
where the time goes in v1:
time: 111 us; the launch traced here: 110 us
  waiting for transfers between devices  53.9 us (49%)
  Pallas kernels  26.3 us (24%)
  starting transfers between devices  24.8 us (22%)
  local copies, waits for them, and re-layouts  3.44 us (3%)
  between operations  1.14 us (1%)
    ppermute x6, waiting for transfers between devices, shards(): lax.ppermute(group[d], 'seq', back(d))  29.2 us
    pallas_call x2, Pallas kernels, attention(): pl.pallas_call(functools.partial(attention_kernel, chips, heads, len(carr...  26.3 us
    ppermute x6, waiting for transfers between devices, shards(): lax.ppermute(part, 'seq', onward(d))  20.6 us
    ppermute x6, starting transfers between devices, shards(): lax.ppermute(part, 'seq', onward(d))  13.5 us
    ppermute x6, starting transfers between devices, shards(): lax.ppermute(group[d], 'seq', back(d))  7.9 us
  transfers between devices with their start and end apart: 19, of which 8 were waited for; matrix products, arithmetic and copies ran while one was open for 1% of the time, Pallas kernels for 24%

profile of v1, /device:TPU:9, one launch (start us, length us, event | category | flops | bytes accessed | tf_op | source)
XLA Modules:
  0.0 110.1 jit_solution(16176562218183752775)
XLA Ops:
  0.7 0.0 copy-start.2
  0.7 0.0 copy-start.3
  0.7 0.0 copy-start.4
  0.7 1.4 %constant_dynamic-slice_fusion.2 = bf16[128,4096]{1,0:T(8,128)(2,1)S(1)} fusion(bf16[128,8192]{1,0:T(8,128)(2,1)} %refs_2_.3, s32[]{:T(128)S(6)} %select_n.85), kind=kLoop, calls=%fused_computation.50 | loop fusion | bytes 2097156 | tf_op jit(solution)/shard_map/dynamic_slice | solution.py:244
  2.1 0.7 collective-permute-start.1
  2.9 0.0 copy-done.2
  2.9 0.1 constant_dynamic-slice_fusion.3
  3.0 0.4 collective-permute-start
  3.4 0.0 copy-done.3
  3.4 0.0 copy-done.4
  3.4 0.1 fusion.9
  3.7 0.2 collective-permute-start.2
  3.9 2.0 %collective-permute-done.2 = bf16[4,128,256]{2,1,0:T(8,128)(2,1)S(1)} collective-permute-done((bf16[4,128,256]{2,1,0:T(8,128)(2,1)S(1)}, bf16[4,128,256]{2,1,0:T(8,128)(2,1)S(1)}, u32[]{:S(2)}, u32[]{:S(2)}) %collective-permute-start.2) | collective-permute-done | bytes 262176 | tf_op jit(solution)/shard_map/ppermute | solution.py:239
  5.9 0.7 collective-permute-start.5
  6.6 4.8 %collective-permute-start.4 = (bf16[2,256,256]{2,1,0:T(8,128)(2,1)S(1)}, bf16[2,256,256]{2,1,0:T(8,128)(2,1)S(1)}, u32[]{:S(2)}, u32[]{:S(2)}) collective-permute-start(bf16[2,256,256]{2,1,0:T(8,128)(2,1)S(1)} %get-tuple-element.54.refs_4_), channel_id=1, source_target_pairs={{0,16},{4,20},{8,24},{12,28},{1,17},{5,21},{9,25},{13,29},{2,18},{... | collective-permute-start | bytes 786440 | tf_op jit(solution)/shard_map/ppermute | solution.py:256
  11.5 1.9 %collective-permute-start.3 = (bf16[2,256,256]{2,1,0:T(8,128)(2,1)S(1)}, bf16[2,256,256]{2,1,0:T(8,128)(2,1)S(1)}, u32[]{:S(2)}, u32[]{:S(2)}) collective-permute-start(bf16[2,256,256]{2,1,0:T(8,128)(2,1)S(1)} %get-tuple-element.54.refs_4_), channel_id=1, source_target_pairs={{0,8},{4,12},{8,16},{12,20},{16,24},{20,28},{1,9},{5,13},{9,17},{1... | collective-permute-start | bytes 786440 | tf_op jit(solution)/shard_map/ppermute | solution.py:256
  13.4 0.1 pad_add_fusion.place
  13.5 0.0 collective-permute-done.5.refs_7_
  13.5 14.9 %collective-permute-done.4.refs_6_ = bf16[2,256,256]{2,1,0:T(8,128)(2,1)S(1)} collective-permute-done((bf16[2,256,256]{2,1,0:T(8,128)(2,1)S(1)}, bf16[2,256,256]{2,1,0:T(8,128)(2,1)S(1)}, u32[]{:S(2)}, u32[]{:S(2)}) %collective-permute-start.4) | collective-permute-done | bytes 262176 | tf_op jit(solution)/shard_map/ppermute | solution.py:256
  28.4 5.6 %collective-permute-done.3.refs_5_ = bf16[2,256,256]{2,1,0:T(8,128)(2,1)S(1)} collective-permute-done((bf16[2,256,256]{2,1,0:T(8,128)(2,1)S(1)}, bf16[2,256,256]{2,1,0:T(8,128)(2,1)S(1)}, u32[]{:S(2)}, u32[]{:S(2)}) %collective-permute-start.3) | collective-permute-done | bytes 262176 | tf_op jit(solution)/shard_map/ppermute | solution.py:256
  34.0 0.7 collective-permute-start.8
  34.7 1.3 %collective-permute-start.7 = (bf16[2,256,256]{2,1,0:T(8,128)(2,1)S(1)}, bf16[2,256,256]{2,1,0:T(8,128)(2,1)S(1)}, u32[]{:S(2)}, u32[]{:S(2)}) collective-permute-start(bf16[2,256,256]{2,1,0:T(8,128)(2,1)S(1)} %get-tuple-element.29.refs_4_), channel_id=1, source_target_pairs={{0,16},{4,20},{8,24},{12,28},{1,17},{5,21},{9,25},{13,29},{2,18},{... | collective-permute-start | bytes 786440 | tf_op jit(solution)/shard_map/ppermute | solution.py:256
  36.0 4.1 %collective-permute-start.6 = (bf16[2,256,256]{2,1,0:T(8,128)(2,1)S(1)}, bf16[2,256,256]{2,1,0:T(8,128)(2,1)S(1)}, u32[]{:S(2)}, u32[]{:S(2)}) collective-permute-start(bf16[2,256,256]{2,1,0:T(8,128)(2,1)S(1)} %get-tuple-element.29.refs_4_), channel_id=1, source_target_pairs={{0,8},{4,12},{8,16},{12,20},{16,24},{20,28},{1,9},{5,13},{9,17},{1... | collective-permute-start | bytes 786440 | tf_op jit(solution)/shard_map/ppermute | solution.py:256
  40.1 0.0 collective-permute-done.1.refs_3_
  40.1 0.0 collective-permute-done.refs_1_
  40.1 13.1 %attention_0.1 = (bf16[128,8192]{1,0:T(8,128)(2,1)}, bf16[128,8192]{1,0:T(8,128)(2,1)}, bf16[128,4096]{1,0:T(8,128)(2,1)}, bf16[128,4096]{1,0:T(8,128)(2,1)}, f3...) custom-call(s32[2]{0:T(128)S(1)} %pad_add_fusion.place, ...), custom_call_target="tpu_custom_call" | custom-call | flops 6442450944 | bytes 6291456 | tf_op jit(solution)/shard_map/attention_0/pallas_call | solution.py:185
  53.2 1.9 %collective-permute-start.9 = (bf16[2,256,256]{2,1,0:T(8,128)(2,1)S(1)}, bf16[2,256,256]{2,1,0:T(8,128)(2,1)S(1)}, u32[]{:S(2)}, u32[]{:S(2)}) collective-permute-start(bf16[2,256,256]{2,1,0:T(8,128)(2,1)S(1)} %get-tuple-element.39), channel_id=1, source_target_pairs={{8,0},{12,4},{16,8},{20,12},{24,16},{28,20},{9,1},{13,5},{17,9},{2... | collective-permute-start | bytes 786440 | tf_op jit(solution)/shard_map/ppermute | solution.py:282
  55.1 1.3 %collective-permute-start.10 = (bf16[2,256,256]{2,1,0:T(8,128)(2,1)S(1)}, bf16[2,256,256]{2,1,0:T(8,128)(2,1)S(1)}, u32[]{:S(2)}, u32[]{:S(2)}) collective-permute-start(bf16[2,256,256]{2,1,0:T(8,128)(2,1)S(1)} %get-tuple-element.40), channel_id=1, source_target_pairs={{16,0},{20,4},{24,8},{28,12},{17,1},{21,5},{25,9},{29,13},{18,2},{... | collective-permute-start | bytes 786440 | tf_op jit(solution)/shard_map/ppermute | solution.py:282
  56.4 0.0 collective-permute-done.8.refs_7_
  56.4 0.7 collective-permute-start.11
  57.1 0.0 collective-permute-done.7.refs_6_
  57.1 0.1 collective-permute-done.6.refs_5_
  57.2 13.3 %attention_2.1 = (bf16[128,8192]{1,0:T(8,128)(2,1)}, bf16[128,8192]{1,0:T(8,128)(2,1)}, bf16[128,4096]{1,0:T(8,128)(2,1)}, bf16[128,4096]{1,0:T(8,128)(2,1)}, f3...) custom-call(s32[2]{0:T(128)S(1)} %pad_add_fusion.place, ...), custom_call_target="tpu_custom_call", output_to_operand_aliasing={{0}: (9, {}), {1}: (10, {}), {2}: (11, {}), {3}: (12, {})} | custom-call | flops 6442450944 | bytes 6291456 | tf_op jit(solution)/shard_map/attention_2/pallas_call | solution.py:185
  70.5 0.8 collective-permute-start.15
  71.3 1.3 %collective-permute-start.16 = (bf16[2,256,256]{2,1,0:T(8,128)(2,1)S(1)}, bf16[2,256,256]{2,1,0:T(8,128)(2,1)S(1)}, u32[]{:S(2)}, u32[]{:S(2)}) collective-permute-start(bf16[2,256,256]{2,1,0:T(8,128)(2,1)S(1)} %get-tuple-element.52), channel_id=1, source_target_pairs={{16,0},{20,4},{24,8},{28,12},{17,1},{21,5},{25,9},{29,13},{18,2},{... | collective-permute-start | bytes 786440 | tf_op jit(solution)/shard_map/ppermute | solution.py:282
  72.6 0.0 collective-permute-done.9
  72.6 1.9 %collective-permute-start.17 = (bf16[2,256,256]{2,1,0:T(8,128)(2,1)S(1)}, bf16[2,256,256]{2,1,0:T(8,128)(2,1)S(1)}, u32[]{:S(2)}, u32[]{:S(2)}) collective-permute-start(bf16[2,256,256]{2,1,0:T(8,128)(2,1)S(1)} %get-tuple-element.53), channel_id=1, source_target_pairs={{8,0},{12,4},{16,8},{20,12},{24,16},{28,20},{9,1},{13,5},{17,9},{2... | collective-permute-start | bytes 786440 | tf_op jit(solution)/shard_map/ppermute | solution.py:282
  74.5 0.0 collective-permute-done.10
  74.5 0.8 collective-permute-start.13
  75.3 0.0 collective-permute-done.11
  75.3 0.0 copy-done
  75.3 0.1 add_convert_fusion.1
  75.4 0.0 copy-start.9
  75.4 0.1 collective-permute-start.14
  75.5 0.0 collective-permute-done.15
  75.5 21.5 %collective-permute-done.16 = bf16[2,256,256]{2,1,0:T(8,128)(2,1)S(1)} collective-permute-done((bf16[2,256,256]{2,1,0:T(8,128)(2,1)S(1)}, bf16[2,256,256]{2,1,0:T(8,128)(2,1)S(1)}, u32[]{:S(2)}, u32[]{:S(2)}) %collective-permute-start.16) | collective-permute-done | bytes 262176 | tf_op jit(solution)/shard_map/ppermute | solution.py:282
  97.0 7.7 %collective-permute-done.17 = bf16[2,256,256]{2,1,0:T(8,128)(2,1)S(1)} collective-permute-done((bf16[2,256,256]{2,1,0:T(8,128)(2,1)S(1)}, bf16[2,256,256]{2,1,0:T(8,128)(2,1)S(1)}, u32[]{:S(2)}, u32[]{:S(2)}) %collective-permute-start.17) | collective-permute-done | bytes 262176 | tf_op jit(solution)/shard_map/ppermute | solution.py:282
  104.7 0.0 copy-done.1
  104.7 0.1 add_convert_fusion
  104.9 0.0 copy-start.7
  104.9 1.1 collective-permute-start.18
  106.0 0.1 collective-permute-start.12
  106.1 0.0 collective-permute-done.14
  106.1 0.8 collective-permute-done.18
  107.1 0.0 copy-start.5
  107.2 0.0 copy-start.6
  107.2 0.0 collective-permute-done.13
  107.2 0.1 constant_dynamic-update-slice_fusion.16
  107.3 0.0 copy-start.10
  107.3 1.3 %collective-permute-done.12 = bf16[128,4096]{1,0:T(8,128)(2,1)S(1)} collective-permute-done((bf16[128,4096]{1,0:T(8,128)(2,1)S(1)}, bf16[128,4096]{1,0:T(8,128)(2,1)S(1)}, u32[]{:S(2)}, u32[]{:S(2)}) %collective-permute-start.12) | collective-permute-done | bytes 1048608 | tf_op jit(solution)/shard_map/ppermute | solution.py:297
  108.6 0.1 constant_dynamic-update-slice_fusion.17
  108.8 0.0 copy-start.8
  108.8 0.0 copy-done.10
  108.8 1.3 %copy-done.8 = bf16[128,8192]{1,0:T(8,128)(2,1)} copy-done((bf16[128,8192]{1,0:T(8,128)(2,1)}, bf16[128,8192]{1,0:T(8,128)(2,1)S(1)}, u32[]{:S(2)}) %copy-start.8) | copy-done | bytes 2097176
  (30 shorter events, 0.4 us)
Async XLA Ops:
  0.7 2.2 %copy-start.2 = (bf16[128,8192]{1,0:T(8,128)(2,1)S(1)}, bf16[128,8192]{1,0:T(8,128)(2,1)}, u32[]{:S(2)}) copy-start(bf16[128,8192]{1,0:T(8,128)(2,1)} %refs_0_.3) | copy-start | bytes 6291460
  0.7 2.7 %copy-start.3 = (bf16[128,1024]{1,0:T(8,128)(2,1)S(1)}, bf16[128,1024]{1,0:T(8,128)(2,1)}, u32[]{:S(2)}) copy-start(bf16[128,1024]{1,0:T(8,128)(2,1)} %param.5) | copy-start | bytes 786436
  0.7 2.7 %copy-start.4 = (bf16[128,1024]{1,0:T(8,128)(2,1)S(1)}, bf16[128,1024]{1,0:T(8,128)(2,1)}, u32[]{:S(2)}) copy-start(bf16[128,1024]{1,0:T(8,128)(2,1)} %param.6) | copy-start | bytes 786436
  2.1 38.0 %collective-permute-start.1 = (bf16[128,4096]{1,0:T(8,128)(2,1)S(1)}, bf16[128,4096]{1,0:T(8,128)(2,1)}, u32[]{:S(2)}, u32[]{:S(2)}) collective-permute-start(bf16[128,4096]{1,0:T(8,128)(2,1)S(1)} %constant_dynamic-slice_fusion.2), channel_id=1, source_target_pairs={{0,4},{4,0},{8,12},{12,8},{16,20},{20,16},{24,28},{28,24},{1,5},{5... | collective-permute-start | bytes 3145736 | tf_op jit(solution)/shard_map/ppermute | solution.py:245
  3.0 37.1 %collective-permute-start = (bf16[128,4096]{1,0:T(8,128)(2,1)S(1)}, bf16[128,4096]{1,0:T(8,128)(2,1)}, u32[]{:S(2)}, u32[]{:S(2)}) collective-permute-start(bf16[128,4096]{1,0:T(8,128)(2,1)S(1)} %constant_dynamic-slice_fusion.3), channel_id=1, source_target_pairs={{0,4},{4,0},{8,12},{12,8},{16,20},{20,16},{24,28},{28,24},{1,5},{5... | collective-permute-start | bytes 3145736 | tf_op jit(solution)/shard_map/ppermute | solution.py:245
  3.7 2.2 %collective-permute-start.2 = (bf16[4,128,256]{2,1,0:T(8,128)(2,1)S(1)}, bf16[4,128,256]{2,1,0:T(8,128)(2,1)S(1)}, u32[]{:S(2)}, u32[]{:S(2)}) collective-permute-start(bf16[4,128,256]{2,1,0:T(8,128)(2,1)S(1)} %get-tuple-element.56), channel_id=1, source_target_pairs={{0,4},{4,0},{8,12},{12,8},{16,20},{20,16},{24,28},{28,24},{1,5},{5... | collective-permute-start | bytes 786440 | tf_op jit(solution)/shard_map/ppermute | solution.py:239
  5.9 7.6 %collective-permute-start.5 = (bf16[2,256,256]{2,1,0:T(8,128)(2,1)S(1)}, bf16[2,256,256]{2,1,0:T(8,128)(2,1)S(1)}, u32[]{:S(2)}, u32[]{:S(2)}) collective-permute-start(bf16[2,256,256]{2,1,0:T(8,128)(2,1)S(1)} %get-tuple-element.54.refs_4_), channel_id=1, source_target_pairs={{0,24},{4,28},{1,25},{5,29},{2,26},{6,30},{3,27},{7,31}} | collective-permute-start | bytes 786440 | tf_op jit(solution)/shard_map/ppermute | solution.py:256
  6.6 21.7 %collective-permute-start.4 = (bf16[2,256,256]{2,1,0:T(8,128)(2,1)S(1)}, bf16[2,256,256]{2,1,0:T(8,128)(2,1)S(1)}, u32[]{:S(2)}, u32[]{:S(2)}) collective-permute-start(bf16[2,256,256]{2,1,0:T(8,128)(2,1)S(1)} %get-tuple-element.54.refs_4_), channel_id=1, source_target_pairs={{0,16},{4,20},{8,24},{12,28},{1,17},{5,21},{9,25},{13,29},{2,18},{... | collective-permute-start | bytes 786440 | tf_op jit(solution)/shard_map/ppermute | solution.py:256
  11.5 22.5 %collective-permute-start.3 = (bf16[2,256,256]{2,1,0:T(8,128)(2,1)S(1)}, bf16[2,256,256]{2,1,0:T(8,128)(2,1)S(1)}, u32[]{:S(2)}, u32[]{:S(2)}) collective-permute-start(bf16[2,256,256]{2,1,0:T(8,128)(2,1)S(1)} %get-tuple-element.54.refs_4_), channel_id=1, source_target_pairs={{0,8},{4,12},{8,16},{12,20},{16,24},{20,28},{1,9},{5,13},{9,17},{1... | collective-permute-start | bytes 786440 | tf_op jit(solution)/shard_map/ppermute | solution.py:256
  34.0 22.4 %collective-permute-start.8 = (bf16[2,256,256]{2,1,0:T(8,128)(2,1)S(1)}, bf16[2,256,256]{2,1,0:T(8,128)(2,1)S(1)}, u32[]{:S(2)}, u32[]{:S(2)}) collective-permute-start(bf16[2,256,256]{2,1,0:T(8,128)(2,1)S(1)} %get-tuple-element.29.refs_4_), channel_id=1, source_target_pairs={{0,24},{4,28},{1,25},{5,29},{2,26},{6,30},{3,27},{7,31}} | collective-permute-start | bytes 786440 | tf_op jit(solution)/shard_map/ppermute | solution.py:256
  34.7 22.4 %collective-permute-start.7 = (bf16[2,256,256]{2,1,0:T(8,128)(2,1)S(1)}, bf16[2,256,256]{2,1,0:T(8,128)(2,1)S(1)}, u32[]{:S(2)}, u32[]{:S(2)}) collective-permute-start(bf16[2,256,256]{2,1,0:T(8,128)(2,1)S(1)} %get-tuple-element.29.refs_4_), channel_id=1, source_target_pairs={{0,16},{4,20},{8,24},{12,28},{1,17},{5,21},{9,25},{13,29},{2,18},{... | collective-permute-start | bytes 786440 | tf_op jit(solution)/shard_map/ppermute | solution.py:256
  36.0 21.2 %collective-permute-start.6 = (bf16[2,256,256]{2,1,0:T(8,128)(2,1)S(1)}, bf16[2,256,256]{2,1,0:T(8,128)(2,1)S(1)}, u32[]{:S(2)}, u32[]{:S(2)}) collective-permute-start(bf16[2,256,256]{2,1,0:T(8,128)(2,1)S(1)} %get-tuple-element.29.refs_4_), channel_id=1, source_target_pairs={{0,8},{4,12},{8,16},{12,20},{16,24},{20,28},{1,9},{5,13},{9,17},{1... | collective-permute-start | bytes 786440 | tf_op jit(solution)/shard_map/ppermute | solution.py:256
  53.2 19.4 %collective-permute-start.9 = (bf16[2,256,256]{2,1,0:T(8,128)(2,1)S(1)}, bf16[2,256,256]{2,1,0:T(8,128)(2,1)S(1)}, u32[]{:S(2)}, u32[]{:S(2)}) collective-permute-start(bf16[2,256,256]{2,1,0:T(8,128)(2,1)S(1)} %get-tuple-element.39), channel_id=1, source_target_pairs={{8,0},{12,4},{16,8},{20,12},{24,16},{28,20},{9,1},{13,5},{17,9},{2... | collective-permute-start | bytes 786440 | tf_op jit(solution)/shard_map/ppermute | solution.py:282
  55.1 19.4 %collective-permute-start.10 = (bf16[2,256,256]{2,1,0:T(8,128)(2,1)S(1)}, bf16[2,256,256]{2,1,0:T(8,128)(2,1)S(1)}, u32[]{:S(2)}, u32[]{:S(2)}) collective-permute-start(bf16[2,256,256]{2,1,0:T(8,128)(2,1)S(1)} %get-tuple-element.40), channel_id=1, source_target_pairs={{16,0},{20,4},{24,8},{28,12},{17,1},{21,5},{25,9},{29,13},{18,2},{... | collective-permute-start | bytes 786440 | tf_op jit(solution)/shard_map/ppermute | solution.py:282
  56.4 18.9 %collective-permute-start.11 = (bf16[2,256,256]{2,1,0:T(8,128)(2,1)S(1)}, bf16[2,256,256]{2,1,0:T(8,128)(2,1)S(1)}, u32[]{:S(2)}, u32[]{:S(2)}) collective-permute-start(bf16[2,256,256]{2,1,0:T(8,128)(2,1)S(1)} %get-tuple-element.41), channel_id=1, source_target_pairs={{24,0},{28,4},{25,1},{29,5},{26,2},{30,6},{27,3},{31,7}} | collective-permute-start | bytes 786440 | tf_op jit(solution)/shard_map/ppermute | solution.py:282
  57.2 18.1 %copy-start = (f32[2,256,256]{2,1,0:T(8,128)S(1)}, f32[2,256,256]{2,1,0:T(8,128)}, u32[]{:S(2)}) copy-start(f32[2,256,256]{2,1,0:T(8,128)} %get-tuple-element.46) | copy-start | bytes 1572868
  70.5 34.3 %copy-start.1 = (f32[2,256,256]{2,1,0:T(8,128)S(1)}, f32[2,256,256]{2,1,0:T(8,128)}, u32[]{:S(2)}) copy-start(f32[2,256,256]{2,1,0:T(8,128)} %get-tuple-element.50) | copy-start | bytes 1572868
  70.5 35.5 %copy-start.11 = (bf16[128,4096]{1,0:T(8,128)(2,1)S(1)}, bf16[128,4096]{1,0:T(8,128)(2,1)}, u32[]{:S(2)}) copy-start(bf16[128,4096]{1,0:T(8,128)(2,1)} %get-tuple-element.43) | copy-start | bytes 3145732
  70.5 5.1 %collective-permute-start.15 = (bf16[2,256,256]{2,1,0:T(8,128)(2,1)S(1)}, bf16[2,256,256]{2,1,0:T(8,128)(2,1)S(1)}, u32[]{:S(2)}, u32[]{:S(2)}) collective-permute-start(bf16[2,256,256]{2,1,0:T(8,128)(2,1)S(1)} %get-tuple-element.51), channel_id=1, source_target_pairs={{24,0},{28,4},{25,1},{29,5},{26,2},{30,6},{27,3},{31,7}} | collective-permute-start | bytes 786440 | tf_op jit(solution)/shard_map/ppermute | solution.py:282
  71.3 25.7 %collective-permute-start.16 = (bf16[2,256,256]{2,1,0:T(8,128)(2,1)S(1)}, bf16[2,256,256]{2,1,0:T(8,128)(2,1)S(1)}, u32[]{:S(2)}, u32[]{:S(2)}) collective-permute-start(bf16[2,256,256]{2,1,0:T(8,128)(2,1)S(1)} %get-tuple-element.52), channel_id=1, source_target_pairs={{16,0},{20,4},{24,8},{28,12},{17,1},{21,5},{25,9},{29,13},{18,2},{... | collective-permute-start | bytes 786440 | tf_op jit(solution)/shard_map/ppermute | solution.py:282
  72.6 32.1 %collective-permute-start.17 = (bf16[2,256,256]{2,1,0:T(8,128)(2,1)S(1)}, bf16[2,256,256]{2,1,0:T(8,128)(2,1)S(1)}, u32[]{:S(2)}, u32[]{:S(2)}) collective-permute-start(bf16[2,256,256]{2,1,0:T(8,128)(2,1)S(1)} %get-tuple-element.53), channel_id=1, source_target_pairs={{8,0},{12,4},{16,8},{20,12},{24,16},{28,20},{9,1},{13,5},{17,9},{2... | collective-permute-start | bytes 786440 | tf_op jit(solution)/shard_map/ppermute | solution.py:282
  74.5 32.6 %collective-permute-start.13 = (bf16[128,4096]{1,0:T(8,128)(2,1)}, bf16[128,4096]{1,0:T(8,128)(2,1)S(1)}, u32[]{:S(2)}, u32[]{:S(2)}) collective-permute-start(bf16[128,4096]{1,0:T(8,128)(2,1)} %get-tuple-element.45), channel_id=1, source_target_pairs={{0,4},{4,0},{8,12},{12,8},{16,20},{20,16},{24,28},{28,24},{1,5},{5... | collective-permute-start | bytes 3145736 | tf_op jit(solution)/shard_map/ppermute | solution.py:297
  75.4 31.8 %copy-start.9 = (bf16[128,8192]{1,0:T(8,128)(2,1)S(1)}, bf16[128,8192]{1,0:T(8,128)(2,1)}, u32[]{:S(2)}) copy-start(bf16[128,8192]{1,0:T(8,128)(2,1)} %get-tuple-element.44) | copy-start | bytes 6291460
  75.4 30.6 %collective-permute-start.14 = (bf16[2,128,256]{2,1,0:T(8,128)(2,1)S(1)}, bf16[2,128,256]{2,1,0:T(8,128)(2,1)S(1)}, u32[]{:S(2)}, u32[]{:S(2)}) collective-permute-start(bf16[2,128,256]{2,1,0:T(8,128)(2,1)S(1)} %slice.209), channel_id=1, source_target_pairs={{0,4},{4,0},{8,12},{12,8},{16,20},{20,16},{24,28},{28,24},{1,5},{5... | collective-permute-start | bytes 393224 | tf_op jit(solution)/shard_map/ppermute | solution.py:293
  104.9 3.8 %copy-start.7 = (bf16[128,8192]{1,0:T(8,128)(2,1)S(1)}, bf16[128,8192]{1,0:T(8,128)(2,1)}, u32[]{:S(2)}) copy-start(bf16[128,8192]{1,0:T(8,128)(2,1)} %get-tuple-element.37) | copy-start | bytes 6291460
  104.9 2.1 %collective-permute-start.18 = (bf16[2,128,256]{2,1,0:T(8,128)(2,1)S(1)}, bf16[2,128,256]{2,1,0:T(8,128)(2,1)S(1)}, u32[]{:S(2)}, u32[]{:S(2)}) collective-permute-start(bf16[2,128,256]{2,1,0:T(8,128)(2,1)S(1)} %slice.216), channel_id=1, source_target_pairs={{0,4},{4,0},{8,12},{12,8},{16,20},{20,16},{24,28},{28,24},{1,5},{5... | collective-permute-start | bytes 393224 | tf_op jit(solution)/shard_map/ppermute | solution.py:293
  106.0 2.7 %collective-permute-start.12 = (bf16[128,4096]{1,0:T(8,128)(2,1)S(1)}, bf16[128,4096]{1,0:T(8,128)(2,1)S(1)}, u32[]{:S(2)}, u32[]{:S(2)}) collective-permute-start(bf16[128,4096]{1,0:T(8,128)(2,1)S(1)} %copy-done.11), channel_id=1, source_target_pairs={{0,4},{4,0},{8,12},{12,8},{16,20},{20,16},{24,28},{28,24},{1,5},{5... | collective-permute-start | bytes 3145736 | tf_op jit(solution)/shard_map/ppermute | solution.py:297
  107.1 1.6 %copy-start.5 = (bf16[128,1024]{1,0:T(8,128)(2,1)}, bf16[128,1024]{1,0:T(8,128)(2,1)S(1)}, u32[]{:S(2)}) copy-start(bf16[128,1024]{1,0:T(8,128)(2,1)S(1)} %get-tuple-element.82) | copy-start | bytes 786436
  107.2 1.6 %copy-start.6 = (bf16[128,1024]{1,0:T(8,128)(2,1)}, bf16[128,1024]{1,0:T(8,128)(2,1)S(1)}, u32[]{:S(2)}) copy-start(bf16[128,1024]{1,0:T(8,128)(2,1)S(1)} %get-tuple-element.83) | copy-start | bytes 786436
  107.3 1.5 %copy-start.10 = (bf16[128,8192]{1,0:T(8,128)(2,1)}, bf16[128,8192]{1,0:T(8,128)(2,1)S(1)}, u32[]{:S(2)}) copy-start(bf16[128,8192]{1,0:T(8,128)(2,1)S(1)} %constant_dynamic-update-slice_fusion.16) | copy-start | bytes 6291460
  108.8 1.3 %copy-start.8 = (bf16[128,8192]{1,0:T(8,128)(2,1)}, bf16[128,8192]{1,0:T(8,128)(2,1)S(1)}, u32[]{:S(2)}) copy-start(bf16[128,8192]{1,0:T(8,128)(2,1)S(1)} %constant_dynamic-update-slice_fusion.17) | copy-start | bytes 6291460

commit v2 on v1

--- a/solution.py
+++ b/solution.py
@@ -241,10 +241,9 @@
     half = query.shape[1] // CORES
 
     def other(tensor):
-        piece = lax.dynamic_slice_in_dim(tensor, (1 - core) * half, half, 1)
-        return lax.ppermute(piece, "seq", sibling)
-
-    query_sib, grad_sib = other(query), other(out_grad)
+        return lax.dynamic_slice_in_dim(tensor, (1 - core) * half, half, 1)
+
+    halves = other(query), other(out_grad)
 
     kv = {}
     first = 0
@@ -254,6 +253,9 @@
             part, *arrived = lax.optimization_barrier((part, *blocks[1:]))
             blocks[1:] = arrived
         blocks = [part] + [lax.ppermute(part, "seq", onward(d)) for d in range(1, chips)]
+        if not first:
+            *halves, blocks[1:] = lax.optimization_barrier((*halves, blocks[1:]))
+            query_sib, grad_sib = (lax.ppermute(h, "seq", sibling) for h in halves)
         for h in range(count):
             kv[first + h] = (h, blocks)
         first += count

time: 111 us -> 109 us (0.982)
  waiting for transfers between devices: 53.9 us -> 51.5 us
    ppermute x6, waiting for transfers between devices: 20.6 us -> 19 us  [shards(): lax.ppermute(part, 'seq', onward(d))]
  transfers between devices with their start and end apart: 19 -> 19, of which waited for: 8 -> 8; matrix products, arithmetic and copies ran while one was open for 1% -> 2% of each run, Pallas kernels for 24% -> 24%
where the time goes in v2:
time: 109 us
  waiting for transfers between devices  51.5 us (47%)
  Pallas kernels  26.3 us (24%)
  starting transfers between devices  24.7 us (23%)
  local copies, waits for them, and re-layouts  4.52 us (4%)
  between operations  1.09 us (1%)
    ppermute x6, waiting for transfers between devices, shards(): lax.ppermute(group[d], 'seq', back(d))  29.2 us
    pallas_call x2, Pallas kernels, attention(): pl.pallas_call(functools.partial(attention_kernel, chips, heads, len(carr...  26.3 us
    ppermute x6, waiting for transfers between devices, shards(): lax.ppermute(part, 'seq', onward(d))  19 us
    ppermute x6, starting transfers between devices, shards(): lax.ppermute(part, 'seq', onward(d))  13.5 us
    ppermute x6, starting transfers between devices, shards(): lax.ppermute(group[d], 'seq', back(d))  7.9 us
  transfers between devices with their start and end apart: 19, of which 8 were waited for; matrix products, arithmetic and copies ran while one was open for 2% of the time, Pallas kernels for 24%

profile of v2, /device:TPU:9, one launch (start us, length us, event | category | flops | bytes accessed | tf_op | source)
XLA Modules:
  0.0 108.6 jit_solution(13122886685870213326)
XLA Ops:
  0.7 1.1 fusion.9
  1.9 0.7 collective-permute-start
  2.6 1.2 %collective-permute-done = bf16[4,128,256]{2,1,0:T(8,128)(2,1)S(1)} collective-permute-done((bf16[4,128,256]{2,1,0:T(8,128)(2,1)S(1)}, bf16[4,128,256]{2,1,0:T(8,128)(2,1)S(1)}, u32[]{:S(2)}, u32[]{:S(2)}) %collective-permute-start) | collective-permute-done | bytes 262176 | tf_op jit(solution)/shard_map/ppermute | solution.py:239
  3.8 0.7 collective-permute-start.3
  4.5 4.8 %collective-permute-start.2 = (bf16[2,256,256]{2,1,0:T(8,128)(2,1)S(1)}, bf16[2,256,256]{2,1,0:T(8,128)(2,1)S(1)}, u32[]{:S(2)}, u32[]{:S(2)}) collective-permute-start(bf16[2,256,256]{2,1,0:T(8,128)(2,1)S(1)} %get-tuple-element.65.refs_4_), channel_id=1, source_target_pairs={{0,16},{4,20},{8,24},{12,28},{1,17},{5,21},{9,25},{13,29},{2,18},{... | collective-permute-start | bytes 786440 | tf_op jit(solution)/shard_map/ppermute | solution.py:255
  9.4 1.9 %collective-permute-start.1 = (bf16[2,256,256]{2,1,0:T(8,128)(2,1)S(1)}, bf16[2,256,256]{2,1,0:T(8,128)(2,1)S(1)}, u32[]{:S(2)}, u32[]{:S(2)}) collective-permute-start(bf16[2,256,256]{2,1,0:T(8,128)(2,1)S(1)} %get-tuple-element.65.refs_4_), channel_id=1, source_target_pairs={{0,8},{4,12},{8,16},{12,20},{16,24},{20,28},{1,9},{5,13},{9,17},{1... | collective-permute-start | bytes 786440 | tf_op jit(solution)/shard_map/ppermute | solution.py:255
  11.3 1.7 %constant_dynamic-slice_fusion.2 = (bf16[128,4096]{1,0:T(8,128)(2,1)S(1)}, bf16[128,4096]{1,0:T(8,128)(2,1)S(1)}) fusion(bf16[128,8192]{1,0:T(8,128)(2,1)} %refs_2_.3, s32[]{:T(128)S(6)} %select_n.85, bf16[128,8192]{1,0:T(8,128)(2,1)} %refs_0_.3), kind=kLoop, calls=%fused_computation.50 | loop fusion | bytes 4194308 | tf_op jit(solution)/shard_map/dynamic_slice | solution.py:244
  13.0 0.0 collective-permute-done.3.refs_7_
  13.0 13.3 %collective-permute-done.2.refs_6_ = bf16[2,256,256]{2,1,0:T(8,128)(2,1)S(1)} collective-permute-done((bf16[2,256,256]{2,1,0:T(8,128)(2,1)S(1)}, bf16[2,256,256]{2,1,0:T(8,128)(2,1)S(1)}, u32[]{:S(2)}, u32[]{:S(2)}) %collective-permute-start.2) | collective-permute-done | bytes 262176 | tf_op jit(solution)/shard_map/ppermute | solution.py:255
  26.3 5.6 %collective-permute-done.1.refs_5_ = bf16[2,256,256]{2,1,0:T(8,128)(2,1)S(1)} collective-permute-done((bf16[2,256,256]{2,1,0:T(8,128)(2,1)S(1)}, bf16[2,256,256]{2,1,0:T(8,128)(2,1)S(1)}, u32[]{:S(2)}, u32[]{:S(2)}) %collective-permute-start.1) | collective-permute-done | bytes 262176 | tf_op jit(solution)/shard_map/ppermute | solution.py:255
  31.9 0.5 collective-permute-start.4
  32.4 0.0 collective-permute-start.5
  32.4 0.1 pad_add_fusion.place
  32.5 0.7 collective-permute-start.8
  33.2 1.3 %collective-permute-start.7 = (bf16[2,256,256]{2,1,0:T(8,128)(2,1)S(1)}, bf16[2,256,256]{2,1,0:T(8,128)(2,1)S(1)}, u32[]{:S(2)}, u32[]{:S(2)}) collective-permute-start(bf16[2,256,256]{2,1,0:T(8,128)(2,1)S(1)} %get-tuple-element.39.refs_4_), channel_id=1, source_target_pairs={{0,16},{4,20},{8,24},{12,28},{1,17},{5,21},{9,25},{13,29},{2,18},{... | collective-permute-start | bytes 786440 | tf_op jit(solution)/shard_map/ppermute | solution.py:255
  34.5 4.1 %collective-permute-start.6 = (bf16[2,256,256]{2,1,0:T(8,128)(2,1)S(1)}, bf16[2,256,256]{2,1,0:T(8,128)(2,1)S(1)}, u32[]{:S(2)}, u32[]{:S(2)}) collective-permute-start(bf16[2,256,256]{2,1,0:T(8,128)(2,1)S(1)} %get-tuple-element.39.refs_4_), channel_id=1, source_target_pairs={{0,8},{4,12},{8,16},{12,20},{16,24},{20,28},{1,9},{5,13},{9,17},{1... | collective-permute-start | bytes 786440 | tf_op jit(solution)/shard_map/ppermute | solution.py:255
  38.6 0.0 collective-permute-done.4.refs_1_
  38.6 0.0 collective-permute-done.5.refs_3_
  38.6 13.1 %attention_0.1 = (bf16[128,8192]{1,0:T(8,128)(2,1)}, bf16[128,8192]{1,0:T(8,128)(2,1)}, bf16[128,4096]{1,0:T(8,128)(2,1)}, bf16[128,4096]{1,0:T(8,128)(2,1)}, f3...) custom-call(s32[2]{0:T(128)S(1)} %pad_add_fusion.place, ...), custom_call_target="tpu_custom_call" | custom-call | flops 6442450944 | bytes 6291456 | tf_op jit(solution)/shard_map/attention_0/pallas_call | solution.py:185
  51.6 1.9 %collective-permute-start.9 = (bf16[2,256,256]{2,1,0:T(8,128)(2,1)S(1)}, bf16[2,256,256]{2,1,0:T(8,128)(2,1)S(1)}, u32[]{:S(2)}, u32[]{:S(2)}) collective-permute-start(bf16[2,256,256]{2,1,0:T(8,128)(2,1)S(1)} %get-tuple-element.49), channel_id=1, source_target_pairs={{8,0},{12,4},{16,8},{20,12},{24,16},{28,20},{9,1},{13,5},{17,9},{2... | collective-permute-start | bytes 786440 | tf_op jit(solution)/shard_map/ppermute | solution.py:284
  53.6 1.3 %collective-permute-start.10 = (bf16[2,256,256]{2,1,0:T(8,128)(2,1)S(1)}, bf16[2,256,256]{2,1,0:T(8,128)(2,1)S(1)}, u32[]{:S(2)}, u32[]{:S(2)}) collective-permute-start(bf16[2,256,256]{2,1,0:T(8,128)(2,1)S(1)} %get-tuple-element.50), channel_id=1, source_target_pairs={{16,0},{20,4},{24,8},{28,12},{17,1},{21,5},{25,9},{29,13},{18,2},{... | collective-permute-start | bytes 786440 | tf_op jit(solution)/shard_map/ppermute | solution.py:284
  54.9 0.0 collective-permute-done.8.refs_7_
  54.9 0.7 collective-permute-start.11
  55.6 0.0 collective-permute-done.7.refs_6_
  55.6 0.1 collective-permute-done.6.refs_5_
  55.7 0.0 copy-start
  55.7 13.3 %attention_2.1 = (bf16[128,8192]{1,0:T(8,128)(2,1)}, bf16[128,8192]{1,0:T(8,128)(2,1)}, bf16[128,4096]{1,0:T(8,128)(2,1)}, bf16[128,4096]{1,0:T(8,128)(2,1)}, f3...) custom-call(s32[2]{0:T(128)S(1)} %pad_add_fusion.place, ...), custom_call_target="tpu_custom_call", output_to_operand_aliasing={{0}: (9, {}), {1}: (10, {}), {2}: (11, {}), {3}: (12, {})} | custom-call | flops 6442450944 | bytes 6291456 | tf_op jit(solution)/shard_map/attention_2/pallas_call | solution.py:185
  69.0 0.0 copy-start.1
  69.0 0.8 collective-permute-start.15
  69.8 1.3 %collective-permute-start.16 = (bf16[2,256,256]{2,1,0:T(8,128)(2,1)S(1)}, bf16[2,256,256]{2,1,0:T(8,128)(2,1)S(1)}, u32[]{:S(2)}, u32[]{:S(2)}) collective-permute-start(bf16[2,256,256]{2,1,0:T(8,128)(2,1)S(1)} %get-tuple-element.62), channel_id=1, source_target_pairs={{16,0},{20,4},{24,8},{28,12},{17,1},{21,5},{25,9},{29,13},{18,2},{... | collective-permute-start | bytes 786440 | tf_op jit(solution)/shard_map/ppermute | solution.py:284
  71.1 0.0 collective-permute-done.9
  71.1 1.9 %collective-permute-start.17 = (bf16[2,256,256]{2,1,0:T(8,128)(2,1)S(1)}, bf16[2,256,256]{2,1,0:T(8,128)(2,1)S(1)}, u32[]{:S(2)}, u32[]{:S(2)}) collective-permute-start(bf16[2,256,256]{2,1,0:T(8,128)(2,1)S(1)} %get-tuple-element.63), channel_id=1, source_target_pairs={{8,0},{12,4},{16,8},{20,12},{24,16},{28,20},{9,1},{13,5},{17,9},{2... | collective-permute-start | bytes 786440 | tf_op jit(solution)/shard_map/ppermute | solution.py:284
  73.0 0.0 collective-permute-done.10
  73.0 0.7 collective-permute-start.13
  73.8 0.0 collective-permute-done.11
  73.8 0.0 copy-done
  73.8 0.1 add_convert_fusion.1
  73.9 0.0 copy-start.6
  73.9 0.1 collective-permute-start.14
  74.0 0.0 collective-permute-done.15
  74.0 21.5 %collective-permute-done.16 = bf16[2,256,256]{2,1,0:T(8,128)(2,1)S(1)} collective-permute-done((bf16[2,256,256]{2,1,0:T(8,128)(2,1)S(1)}, bf16[2,256,256]{2,1,0:T(8,128)(2,1)S(1)}, u32[]{:S(2)}, u32[]{:S(2)}) %collective-permute-start.16) | collective-permute-done | bytes 262176 | tf_op jit(solution)/shard_map/ppermute | solution.py:284
  95.5 7.7 %collective-permute-done.17 = bf16[2,256,256]{2,1,0:T(8,128)(2,1)S(1)} collective-permute-done((bf16[2,256,256]{2,1,0:T(8,128)(2,1)S(1)}, bf16[2,256,256]{2,1,0:T(8,128)(2,1)S(1)}, u32[]{:S(2)}, u32[]{:S(2)}) %collective-permute-start.17) | collective-permute-done | bytes 262176 | tf_op jit(solution)/shard_map/ppermute | solution.py:284
  103.2 0.0 copy-done.1
  103.2 0.1 add_convert_fusion
  103.4 0.0 copy-start.4
  103.4 1.1 collective-permute-start.18
  104.5 0.0 copy-done.8
  104.5 0.1 collective-permute-start.12
  104.6 0.0 collective-permute-done.14
  104.6 0.8 collective-permute-done.18
  105.6 0.0 copy-start.2
  105.6 0.0 copy-start.3
  105.7 0.0 collective-permute-done.13
  105.7 0.0 copy-done.6
  105.7 0.1 constant_dynamic-update-slice_fusion.16
  105.8 0.0 copy-start.7
  105.8 1.3 %collective-permute-done.12 = bf16[128,4096]{1,0:T(8,128)(2,1)S(1)} collective-permute-done((bf16[128,4096]{1,0:T(8,128)(2,1)S(1)}, bf16[128,4096]{1,0:T(8,128)(2,1)S(1)}, u32[]{:S(2)}, u32[]{:S(2)}) %collective-permute-start.12) | collective-permute-done | bytes 1048608 | tf_op jit(solution)/shard_map/ppermute | solution.py:299
  107.1 0.0 copy-done.4
  107.1 0.1 constant_dynamic-update-slice_fusion.17
  107.2 0.0 copy-done.2
  107.3 0.0 copy-done.3
  107.3 0.0 copy-start.5
  107.3 0.0 copy-done.7
  107.3 1.3 %copy-done.5 = bf16[128,8192]{1,0:T(8,128)(2,1)} copy-done((bf16[128,8192]{1,0:T(8,128)(2,1)}, bf16[128,8192]{1,0:T(8,128)(2,1)S(1)}, u32[]{:S(2)}) %copy-start.5) | copy-done | bytes 2097176
  (23 shorter events, 0.4 us)
Async XLA Ops:
  1.9 1.9 %collective-permute-start = (bf16[4,128,256]{2,1,0:T(8,128)(2,1)S(1)}, bf16[4,128,256]{2,1,0:T(8,128)(2,1)S(1)}, u32[]{:S(2)}, u32[]{:S(2)}) collective-permute-start(bf16[4,128,256]{2,1,0:T(8,128)(2,1)S(1)} %get-tuple-element.66), channel_id=1, source_target_pairs={{0,4},{4,0},{8,12},{12,8},{16,20},{20,16},{24,28},{28,24},{1,5},{5... | collective-permute-start | bytes 786440 | tf_op jit(solution)/shard_map/ppermute | solution.py:239
  3.8 9.2 %collective-permute-start.3 = (bf16[2,256,256]{2,1,0:T(8,128)(2,1)S(1)}, bf16[2,256,256]{2,1,0:T(8,128)(2,1)S(1)}, u32[]{:S(2)}, u32[]{:S(2)}) collective-permute-start(bf16[2,256,256]{2,1,0:T(8,128)(2,1)S(1)} %get-tuple-element.65.refs_4_), channel_id=1, source_target_pairs={{0,24},{4,28},{1,25},{5,29},{2,26},{6,30},{3,27},{7,31}} | collective-permute-start | bytes 786440 | tf_op jit(solution)/shard_map/ppermute | solution.py:255
  4.5 21.7 %collective-permute-start.2 = (bf16[2,256,256]{2,1,0:T(8,128)(2,1)S(1)}, bf16[2,256,256]{2,1,0:T(8,128)(2,1)S(1)}, u32[]{:S(2)}, u32[]{:S(2)}) collective-permute-start(bf16[2,256,256]{2,1,0:T(8,128)(2,1)S(1)} %get-tuple-element.65.refs_4_), channel_id=1, source_target_pairs={{0,16},{4,20},{8,24},{12,28},{1,17},{5,21},{9,25},{13,29},{2,18},{... | collective-permute-start | bytes 786440 | tf_op jit(solution)/shard_map/ppermute | solution.py:255
  9.4 22.5 %collective-permute-start.1 = (bf16[2,256,256]{2,1,0:T(8,128)(2,1)S(1)}, bf16[2,256,256]{2,1,0:T(8,128)(2,1)S(1)}, u32[]{:S(2)}, u32[]{:S(2)}) collective-permute-start(bf16[2,256,256]{2,1,0:T(8,128)(2,1)S(1)} %get-tuple-element.65.refs_4_), channel_id=1, source_target_pairs={{0,8},{4,12},{8,16},{12,20},{16,24},{20,28},{1,9},{5,13},{9,17},{1... | collective-permute-start | bytes 786440 | tf_op jit(solution)/shard_map/ppermute | solution.py:255
  31.9 6.7 %collective-permute-start.4 = (bf16[128,4096]{1,0:T(8,128)(2,1)S(1)}, bf16[128,4096]{1,0:T(8,128)(2,1)}, u32[]{:S(2)}, u32[]{:S(2)}) collective-permute-start(bf16[128,4096]{1,0:T(8,128)(2,1)S(1)} %get-tuple-element.34), channel_id=1, source_target_pairs={{0,4},{4,0},{8,12},{12,8},{16,20},{20,16},{24,28},{28,24},{1,5},{5... | collective-permute-start | bytes 3145736 | tf_op jit(solution)/shard_map/ppermute | solution.py:258
  32.4 6.2 %collective-permute-start.5 = (bf16[128,4096]{1,0:T(8,128)(2,1)S(1)}, bf16[128,4096]{1,0:T(8,128)(2,1)}, u32[]{:S(2)}, u32[]{:S(2)}) collective-permute-start(bf16[128,4096]{1,0:T(8,128)(2,1)S(1)} %get-tuple-element.35), channel_id=1, source_target_pairs={{0,4},{4,0},{8,12},{12,8},{16,20},{20,16},{24,28},{28,24},{1,5},{5... | collective-permute-start | bytes 3145736 | tf_op jit(solution)/shard_map/ppermute | solution.py:258
  32.5 22.4 %collective-permute-start.8 = (bf16[2,256,256]{2,1,0:T(8,128)(2,1)S(1)}, bf16[2,256,256]{2,1,0:T(8,128)(2,1)S(1)}, u32[]{:S(2)}, u32[]{:S(2)}) collective-permute-start(bf16[2,256,256]{2,1,0:T(8,128)(2,1)S(1)} %get-tuple-element.39.refs_4_), channel_id=1, source_target_pairs={{0,24},{4,28},{1,25},{5,29},{2,26},{6,30},{3,27},{7,31}} | collective-permute-start | bytes 786440 | tf_op jit(solution)/shard_map/ppermute | solution.py:255
  33.2 22.4 %collective-permute-start.7 = (bf16[2,256,256]{2,1,0:T(8,128)(2,1)S(1)}, bf16[2,256,256]{2,1,0:T(8,128)(2,1)S(1)}, u32[]{:S(2)}, u32[]{:S(2)}) collective-permute-start(bf16[2,256,256]{2,1,0:T(8,128)(2,1)S(1)} %get-tuple-element.39.refs_4_), channel_id=1, source_target_pairs={{0,16},{4,20},{8,24},{12,28},{1,17},{5,21},{9,25},{13,29},{2,18},{... | collective-permute-start | bytes 786440 | tf_op jit(solution)/shard_map/ppermute | solution.py:255
  34.5 21.2 %collective-permute-start.6 = (bf16[2,256,256]{2,1,0:T(8,128)(2,1)S(1)}, bf16[2,256,256]{2,1,0:T(8,128)(2,1)S(1)}, u32[]{:S(2)}, u32[]{:S(2)}) collective-permute-start(bf16[2,256,256]{2,1,0:T(8,128)(2,1)S(1)} %get-tuple-element.39.refs_4_), channel_id=1, source_target_pairs={{0,8},{4,12},{8,16},{12,20},{16,24},{20,28},{1,9},{5,13},{9,17},{1... | collective-permute-start | bytes 786440 | tf_op jit(solution)/shard_map/ppermute | solution.py:255
  51.6 19.5 %collective-permute-start.9 = (bf16[2,256,256]{2,1,0:T(8,128)(2,1)S(1)}, bf16[2,256,256]{2,1,0:T(8,128)(2,1)S(1)}, u32[]{:S(2)}, u32[]{:S(2)}) collective-permute-start(bf16[2,256,256]{2,1,0:T(8,128)(2,1)S(1)} %get-tuple-element.49), channel_id=1, source_target_pairs={{8,0},{12,4},{16,8},{20,12},{24,16},{28,20},{9,1},{13,5},{17,9},{2... | collective-permute-start | bytes 786440 | tf_op jit(solution)/shard_map/ppermute | solution.py:284
  53.6 19.5 %collective-permute-start.10 = (bf16[2,256,256]{2,1,0:T(8,128)(2,1)S(1)}, bf16[2,256,256]{2,1,0:T(8,128)(2,1)S(1)}, u32[]{:S(2)}, u32[]{:S(2)}) collective-permute-start(bf16[2,256,256]{2,1,0:T(8,128)(2,1)S(1)} %get-tuple-element.50), channel_id=1, source_target_pairs={{16,0},{20,4},{24,8},{28,12},{17,1},{21,5},{25,9},{29,13},{18,2},{... | collective-permute-start | bytes 786440 | tf_op jit(solution)/shard_map/ppermute | solution.py:284
  54.9 18.9 %collective-permute-start.11 = (bf16[2,256,256]{2,1,0:T(8,128)(2,1)S(1)}, bf16[2,256,256]{2,1,0:T(8,128)(2,1)S(1)}, u32[]{:S(2)}, u32[]{:S(2)}) collective-permute-start(bf16[2,256,256]{2,1,0:T(8,128)(2,1)S(1)} %get-tuple-element.51), channel_id=1, source_target_pairs={{24,0},{28,4},{25,1},{29,5},{26,2},{30,6},{27,3},{31,7}} | collective-permute-start | bytes 786440 | tf_op jit(solution)/shard_map/ppermute | solution.py:284
  55.7 18.1 %copy-start = (f32[2,256,256]{2,1,0:T(8,128)S(1)}, f32[2,256,256]{2,1,0:T(8,128)}, u32[]{:S(2)}) copy-start(f32[2,256,256]{2,1,0:T(8,128)} %get-tuple-element.56) | copy-start | bytes 1572868
  69.0 34.2 %copy-start.1 = (f32[2,256,256]{2,1,0:T(8,128)S(1)}, f32[2,256,256]{2,1,0:T(8,128)}, u32[]{:S(2)}) copy-start(f32[2,256,256]{2,1,0:T(8,128)} %get-tuple-element.60) | copy-start | bytes 1572868
  69.0 35.5 %copy-start.8 = (bf16[128,4096]{1,0:T(8,128)(2,1)S(1)}, bf16[128,4096]{1,0:T(8,128)(2,1)}, u32[]{:S(2)}) copy-start(bf16[128,4096]{1,0:T(8,128)(2,1)} %get-tuple-element.53) | copy-start | bytes 3145732
  69.0 5.1 %collective-permute-start.15 = (bf16[2,256,256]{2,1,0:T(8,128)(2,1)S(1)}, bf16[2,256,256]{2,1,0:T(8,128)(2,1)S(1)}, u32[]{:S(2)}, u32[]{:S(2)}) collective-permute-start(bf16[2,256,256]{2,1,0:T(8,128)(2,1)S(1)} %get-tuple-element.61), channel_id=1, source_target_pairs={{24,0},{28,4},{25,1},{29,5},{26,2},{30,6},{27,3},{31,7}} | collective-permute-start | bytes 786440 | tf_op jit(solution)/shard_map/ppermute | solution.py:284
  69.8 25.7 %collective-permute-start.16 = (bf16[2,256,256]{2,1,0:T(8,128)(2,1)S(1)}, bf16[2,256,256]{2,1,0:T(8,128)(2,1)S(1)}, u32[]{:S(2)}, u32[]{:S(2)}) collective-permute-start(bf16[2,256,256]{2,1,0:T(8,128)(2,1)S(1)} %get-tuple-element.62), channel_id=1, source_target_pairs={{16,0},{20,4},{24,8},{28,12},{17,1},{21,5},{25,9},{29,13},{18,2},{... | collective-permute-start | bytes 786440 | tf_op jit(solution)/shard_map/ppermute | solution.py:284
  71.1 32.1 %collective-permute-start.17 = (bf16[2,256,256]{2,1,0:T(8,128)(2,1)S(1)}, bf16[2,256,256]{2,1,0:T(8,128)(2,1)S(1)}, u32[]{:S(2)}, u32[]{:S(2)}) collective-permute-start(bf16[2,256,256]{2,1,0:T(8,128)(2,1)S(1)} %get-tuple-element.63), channel_id=1, source_target_pairs={{8,0},{12,4},{16,8},{20,12},{24,16},{28,20},{9,1},{13,5},{17,9},{2... | collective-permute-start | bytes 786440 | tf_op jit(solution)/shard_map/ppermute | solution.py:284
  73.0 32.6 %collective-permute-start.13 = (bf16[128,4096]{1,0:T(8,128)(2,1)}, bf16[128,4096]{1,0:T(8,128)(2,1)S(1)}, u32[]{:S(2)}, u32[]{:S(2)}) collective-permute-start(bf16[128,4096]{1,0:T(8,128)(2,1)} %get-tuple-element.55), channel_id=1, source_target_pairs={{0,4},{4,0},{8,12},{12,8},{16,20},{20,16},{24,28},{28,24},{1,5},{5... | collective-permute-start | bytes 3145736 | tf_op jit(solution)/shard_map/ppermute | solution.py:299
  73.9 31.8 %copy-start.6 = (bf16[128,8192]{1,0:T(8,128)(2,1)S(1)}, bf16[128,8192]{1,0:T(8,128)(2,1)}, u32[]{:S(2)}) copy-start(bf16[128,8192]{1,0:T(8,128)(2,1)} %get-tuple-element.54) | copy-start | bytes 6291460
  73.9 30.6 %collective-permute-start.14 = (bf16[2,128,256]{2,1,0:T(8,128)(2,1)S(1)}, bf16[2,128,256]{2,1,0:T(8,128)(2,1)S(1)}, u32[]{:S(2)}, u32[]{:S(2)}) collective-permute-start(bf16[2,128,256]{2,1,0:T(8,128)(2,1)S(1)} %slice.209), channel_id=1, source_target_pairs={{0,4},{4,0},{8,12},{12,8},{16,20},{20,16},{24,28},{28,24},{1,5},{5... | collective-permute-start | bytes 393224 | tf_op jit(solution)/shard_map/ppermute | solution.py:295
  103.4 3.8 %copy-start.4 = (bf16[128,8192]{1,0:T(8,128)(2,1)S(1)}, bf16[128,8192]{1,0:T(8,128)(2,1)}, u32[]{:S(2)}) copy-start(bf16[128,8192]{1,0:T(8,128)(2,1)} %get-tuple-element.47) | copy-start | bytes 6291460
  103.4 2.1 %collective-permute-start.18 = (bf16[2,128,256]{2,1,0:T(8,128)(2,1)S(1)}, bf16[2,128,256]{2,1,0:T(8,128)(2,1)S(1)}, u32[]{:S(2)}, u32[]{:S(2)}) collective-permute-start(bf16[2,128,256]{2,1,0:T(8,128)(2,1)S(1)} %slice.216), channel_id=1, source_target_pairs={{0,4},{4,0},{8,12},{12,8},{16,20},{20,16},{24,28},{28,24},{1,5},{5... | collective-permute-start | bytes 393224 | tf_op jit(solution)/shard_map/ppermute | solution.py:295
  104.5 2.7 %collective-permute-start.12 = (bf16[128,4096]{1,0:T(8,128)(2,1)S(1)}, bf16[128,4096]{1,0:T(8,128)(2,1)S(1)}, u32[]{:S(2)}, u32[]{:S(2)}) collective-permute-start(bf16[128,4096]{1,0:T(8,128)(2,1)S(1)} %copy-done.8), channel_id=1, source_target_pairs={{0,4},{4,0},{8,12},{12,8},{16,20},{20,16},{24,28},{28,24},{1,5},{5... | collective-permute-start | bytes 3145736 | tf_op jit(solution)/shard_map/ppermute | solution.py:299
  105.6 1.6 %copy-start.2 = (bf16[128,1024]{1,0:T(8,128)(2,1)}, bf16[128,1024]{1,0:T(8,128)(2,1)S(1)}, u32[]{:S(2)}) copy-start(bf16[128,1024]{1,0:T(8,128)(2,1)S(1)} %get-tuple-element.92) | copy-start | bytes 786436
  105.6 1.6 %copy-start.3 = (bf16[128,1024]{1,0:T(8,128)(2,1)}, bf16[128,1024]{1,0:T(8,128)(2,1)S(1)}, u32[]{:S(2)}) copy-start(bf16[128,1024]{1,0:T(8,128)(2,1)S(1)} %get-tuple-element.93) | copy-start | bytes 786436
  105.8 1.5 %copy-start.7 = (bf16[128,8192]{1,0:T(8,128)(2,1)}, bf16[128,8192]{1,0:T(8,128)(2,1)S(1)}, u32[]{:S(2)}) copy-start(bf16[128,8192]{1,0:T(8,128)(2,1)S(1)} %constant_dynamic-update-slice_fusion.16) | copy-start | bytes 6291460
  107.3 1.3 %copy-start.5 = (bf16[128,8192]{1,0:T(8,128)(2,1)}, bf16[128,8192]{1,0:T(8,128)(2,1)S(1)}, u32[]{:S(2)}) copy-start(bf16[128,8192]{1,0:T(8,128)(2,1)S(1)} %constant_dynamic-update-slice_fusion.17) | copy-start | bytes 6291460
